TPU v7x, 256 devices: a whole 4x4x8 slice. The times are simulated.
256 devices in a mesh: band: 8 (over x, y_hi), fft: 32 (over y_lo, z, core).
Axes of the slice: x: 4, y: 4 (y_hi: 2, y_lo: 2; y = y_hi * 2 + y_lo), z: 8, core: 2. Of those that a mesh axis runs over, the one named last changes fastest.
Arguments:
- orbitals: float32 [16, 128, 128, 128], P('band', 'fft'), may hold values from -6 to 6
- owners: int32 [4], replicated, may hold values from 0 to 15, as said below
- kernel: float32 [128, 128, 128], P(None, 'fft'), may hold values from 0.005 to 1, as said below
Outputs:
- exchange: float32 [16, 128, 128, 128], P('band', 'fft')
- projector: float32 [4, 128, 128, 128], P(None, 'fft', 'band')
Inputs may be any that keep to these rules, and one draw needn't show every extreme that they name: `owners`: 4 distinct band indices, 0 and 15 among them. `kernel`: even: the value at indices (a, b, c) equals that at ((-a) mod 128, (-b) mod 128, (-c) mod 128).
All inputs are finite; a program needn't handle non-finite values.
Results may differ from a plain program's by a relative error of at most 0.0001.
Values sent between devices are 32-bit elements; how exact they have to be, the bound alone decides.
A program may use at most 64 MiB of HBM per device.

v0:
```python
import math

import jax
import jax.numpy as jnp
from jax import lax
from jax.sharding import PartitionSpec as P

HIGHEST_PRECISION = lax.Precision.HIGHEST
along_z = "pxyz,zk->pxyk"
along_y = "pxyz,yk->pxkz"
along_x = "pxyz,xk->pkyz"


def broadcast(value, axis, source):
    kept = jnp.where(lax.axis_index(axis) == source, value, 0).astype(value.dtype)
    return lax.psum(kept, axis)


def tables(length):
    counter = jnp.arange(length, dtype=jnp.int32)
    phases = counter[:, None] * counter[None, :] % length
    angles = phases.astype(jnp.float32) * (2.0 * math.pi / length)
    return (jnp.cos(angles), jnp.sin(angles))


def along_axis(values, matrix, einsum_form):
    return jnp.einsum(einsum_form, values, matrix, precision=HIGHEST_PRECISION)


def rotate(real_part, imag_part, cos_table, sin_table, einsum_form, direction_sign):
    real_cos = along_axis(real_part, cos_table, einsum_form)
    real_sin = along_axis(real_part, sin_table, einsum_form)
    imag_cos = along_axis(imag_part, cos_table, einsum_form)
    imag_sin = along_axis(imag_part, sin_table, einsum_form)
    return (real_cos - direction_sign * imag_sin, imag_cos + direction_sign * real_sin)


def potentials(density, kernel, cos_table, sin_table):
    grid_len = density.shape[3]
    real_part = along_axis(density, cos_table, along_z)
    imag_part = -along_axis(density, sin_table, along_z)
    real_part, imag_part = rotate(real_part, imag_part, cos_table, sin_table, along_y, -1.0)
    first_part, second_part = rotate(
        lax.all_to_all(real_part, "fft", split_axis=2, concat_axis=1, tiled=True),
        lax.all_to_all(imag_part, "fft", split_axis=2, concat_axis=1, tiled=True),
        cos_table,
        sin_table,
        along_x,
        -1.0,
    )
    first_part = first_part * kernel[None]
    second_part = second_part * kernel[None]
    first_part, second_part = rotate(first_part, second_part, cos_table, sin_table, along_x, 1.0)
    real_part = lax.all_to_all(first_part, "fft", split_axis=1, concat_axis=2, tiled=True)
    imag_part = lax.all_to_all(second_part, "fft", split_axis=1, concat_axis=2, tiled=True)
    real_part, imag_part = rotate(real_part, imag_part, cos_table, sin_table, along_y, 1.0)
    inverse_norm = 1.0 / float(grid_len**3)
    real_out = along_axis(real_part, cos_table, along_z) - along_axis(imag_part, sin_table, along_z)
    return real_out * inverse_norm


def shards(orbitals, owners, kernel):
    resident = orbitals.shape[0]
    grid_len = orbitals.shape[3]
    count = owners.shape[0]
    cos_table, sin_table = tables(grid_len)
    collected = []
    for position in range(count):
        owner_band = owners[position]
        local_band = lax.dynamic_index_in_dim(orbitals, owner_band % resident, 0, keepdims=False)
        collected.append(broadcast(local_band, "band", owner_band // resident))
    fetched = jnp.stack(collected)
    fields = jnp.stack(
        [
            potentials(fetched[position][None] * orbitals, kernel, cos_table, sin_table)
            for position in range(count)
        ]
    )
    exchange = -jnp.sum(fields * fetched[:, None], axis=0)
    partial_sum = -jnp.sum(fields * orbitals[None], axis=1)
    projector = lax.psum_scatter(partial_sum, "band", scatter_dimension=2, tiled=True)
    return (exchange, projector)


def solution(mesh):
    return jax.shard_map(
        shards,
        mesh=mesh,
        in_specs=(P("band", "fft", None, None), P(), P(None, "fft", None)),
        out_specs=(P("band", "fft", None, None), P(None, "fft", "band", None)),
        check_vma=False,
    )
```

profile of v0, /device:TPU:7, one launch (start us, length us, event | category | flops | bytes accessed | tf_op | source)
XLA Modules:
  0.0 582.5 jit_solution(4413093630539982352)
XLA Ops:
  22.2 89.7 %all-reduce.3.cloned.1.call-done = (f32[4,128,128]{2,1,0:T(8,128)}, f32[4,128,128]{2,1,0:T(8,128)}, f32[4,128,128]{2,1,0:T(8,128)}, f32[4,128,128]{2,1,0:T(8,128)}) async-done(((f32[4,128,128]{2,1,0:T(8,128)}, f32[4,128,128]{2,1,0:T(8,128)}, f32[4,128,128]{2,1,0:T(8,128)}, f32[4,128,128]{2,1,0:T(8,128)}), (f32[4,128,128]{2,1,0:T(8,128)}, f32[4,128,128]{2,1,0:T(8,128)}, f32[4,128,128]{2,1,0:T(8,128)}, ...) | async-done | bytes 1048592 | tf_op jit(solution)/shard_map/psum | solution.py:16
  120.0 13.4 %all-to-all-start = ((f32[2,4,128,128]{3,1,0,2:T(4,128)}), f32[2,4,128,128]{3,1,0,2:T(4,128)}, u32[]{:S(2)}, u32[]{:S(2)}) async-start(f32[2,4,128,128]{3,1,0,2:T(4,128)} %copy.129), calls=%async_computation | async-start | bytes 1048576 | tf_op jit(solution)/shard_map/all_to_all | solution.py:44
  141.3 8.6 %all-to-all-done = f32[2,4,128,128]{3,1,0,2:T(4,128)} async-done(((f32[2,4,128,128]{3,1,0,2:T(4,128)}), f32[2,4,128,128]{3,1,0,2:T(4,128)}, u32[]{:S(2)}, u32[]{:S(2)}) %all-to-all-start) | async-done | bytes 524320 | tf_op jit(solution)/shard_map/all_to_all | solution.py:44
  149.9 5.8 all-to-all-start.1
  159.8 12.6 %all-to-all-done.1 = f32[2,4,128,128]{3,1,0,2:T(4,128)S(1)} async-done(((f32[2,4,128,128]{3,1,0,2:T(4,128)}), f32[2,4,128,128]{3,1,0,2:T(4,128)S(1)}, u32[]{:S(2)}, u32[]{:S(2)}) %all-to-all-start.1) | async-done | bytes 524320 | tf_op jit(solution)/shard_map/all_to_all | solution.py:45
  172.4 6.7 %all-to-all-start.5 = ((f32[2,4,128,128]{3,1,0,2:T(4,128)}), f32[2,4,128,128]{3,1,0,2:T(4,128)}, u32[]{:S(2)}, u32[]{:S(2)}) async-start(f32[2,4,128,128]{3,1,0,2:T(4,128)} %copy.159), calls=%async_computation.5 | async-start | bytes 1048576 | tf_op jit(solution)/shard_map/all_to_all | solution.py:45
  183.3 12.3 %all-to-all-done.5 = f32[2,4,128,128]{3,1,0,2:T(4,128)} async-done(((f32[2,4,128,128]{3,1,0,2:T(4,128)}), f32[2,4,128,128]{3,1,0,2:T(4,128)}, u32[]{:S(2)}, u32[]{:S(2)}) %all-to-all-start.5) | async-done | bytes 524320 | tf_op jit(solution)/shard_map/all_to_all | solution.py:45
  195.6 6.3 %all-to-all-start.4 = ((f32[2,4,128,128]{3,1,0,2:T(4,128)}), f32[2,4,128,128]{3,1,0,2:T(4,128)}, u32[]{:S(2)}, u32[]{:S(2)}) async-start(f32[2,4,128,128]{3,1,0,2:T(4,128)} %copy.154), calls=%async_computation.4 | async-start | bytes 1048576 | tf_op jit(solution)/shard_map/all_to_all | solution.py:44
  212.4 6.3 %all-to-all-done.4 = f32[2,4,128,128]{3,1,0,2:T(4,128)} async-done(((f32[2,4,128,128]{3,1,0,2:T(4,128)}), f32[2,4,128,128]{3,1,0,2:T(4,128)}, u32[]{:S(2)}, u32[]{:S(2)}) %all-to-all-start.4) | async-done | bytes 524320 | tf_op jit(solution)/shard_map/all_to_all | solution.py:44
  218.7 6.1 %all-to-all-start.9 = ((f32[2,4,128,128]{3,1,0,2:T(4,128)}), f32[2,4,128,128]{3,1,0,2:T(4,128)S(1)}, u32[]{:S(2)}, u32[]{:S(2)}) async-start(f32[2,4,128,128]{3,1,0,2:T(4,128)} %copy.183), calls=%async_computation.9 | async-start | bytes 1048576 | tf_op jit(solution)/shard_map/all_to_all | solution.py:45
  228.4 13.0 %all-to-all-done.9 = f32[2,4,128,128]{3,1,0,2:T(4,128)S(1)} async-done(((f32[2,4,128,128]{3,1,0,2:T(4,128)}), f32[2,4,128,128]{3,1,0,2:T(4,128)S(1)}, u32[]{:S(2)}, u32[]{:S(2)}) %all-to-all-start.9) | async-done | bytes 524320 | tf_op jit(solution)/shard_map/all_to_all | solution.py:45
  241.4 5.7 all-to-all-start.8
  255.2 8.7 %all-to-all-done.8 = f32[2,4,128,128]{3,1,0,2:T(4,128)S(1)} async-done(((f32[2,4,128,128]{3,1,0,2:T(4,128)}), f32[2,4,128,128]{3,1,0,2:T(4,128)S(1)}, u32[]{:S(2)}, u32[]{:S(2)}) %all-to-all-start.8) | async-done | bytes 524320 | tf_op jit(solution)/shard_map/all_to_all | solution.py:44
  273.8 13.2 %all-to-all-done.13 = f32[2,4,128,128]{3,1,0,2:T(4,128)S(1)} async-done(((f32[2,4,128,128]{3,1,0,2:T(4,128)}), f32[2,4,128,128]{3,1,0,2:T(4,128)S(1)}, u32[]{:S(2)}, u32[]{:S(2)}) %all-to-all-start.13) | async-done | bytes 524320 | tf_op jit(solution)/shard_map/all_to_all | solution.py:45
  287.0 6.6 %all-to-all-start.12 = ((f32[2,4,128,128]{3,1,0,2:T(4,128)}), f32[2,4,128,128]{3,1,0,2:T(4,128)}, u32[]{:S(2)}, u32[]{:S(2)}) async-start(f32[2,4,128,128]{3,1,0,2:T(4,128)} %copy.202), calls=%async_computation.12 | async-start | bytes 1048576 | tf_op jit(solution)/shard_map/all_to_all | solution.py:44
  299.6 10.6 %all-to-all-done.12 = f32[2,4,128,128]{3,1,0,2:T(4,128)} async-done(((f32[2,4,128,128]{3,1,0,2:T(4,128)}), f32[2,4,128,128]{3,1,0,2:T(4,128)}, u32[]{:S(2)}, u32[]{:S(2)}) %all-to-all-start.12) | async-done | bytes 524320 | tf_op jit(solution)/shard_map/all_to_all | solution.py:44
  310.2 5.7 all-to-all-start.2
  319.5 13.2 %all-to-all-done.2 = f32[2,128,4,128]{3,2,0,1:T(4,128)S(1)} async-done(((f32[2,128,4,128]{3,2,0,1:T(4,128)}), f32[2,128,4,128]{3,2,0,1:T(4,128)S(1)}, u32[]{:S(2)}, u32[]{:S(2)}) %all-to-all-start.2) | async-done | bytes 524320 | tf_op jit(solution)/shard_map/all_to_all | solution.py:54
  332.6 6.7 %all-to-all-start.3 = ((f32[2,128,4,128]{3,2,0,1:T(4,128)}), f32[2,128,4,128]{3,2,0,1:T(4,128)}, u32[]{:S(2)}, u32[]{:S(2)}) async-start(f32[2,128,4,128]{3,2,0,1:T(4,128)} %copy.147), calls=%async_computation.3 | async-start | bytes 1048576 | tf_op jit(solution)/shard_map/all_to_all | solution.py:55
  346.3 9.6 %all-to-all-done.3 = f32[2,128,4,128]{3,2,0,1:T(4,128)} async-done(((f32[2,128,4,128]{3,2,0,1:T(4,128)}), f32[2,128,4,128]{3,2,0,1:T(4,128)}, u32[]{:S(2)}, u32[]{:S(2)}) %all-to-all-start.3) | async-done | bytes 524320 | tf_op jit(solution)/shard_map/all_to_all | solution.py:55
  355.9 5.7 all-to-all-start.7
  365.1 13.2 %all-to-all-done.7 = f32[2,128,4,128]{3,2,0,1:T(4,128)S(1)} async-done(((f32[2,128,4,128]{3,2,0,1:T(4,128)}), f32[2,128,4,128]{3,2,0,1:T(4,128)S(1)}, u32[]{:S(2)}, u32[]{:S(2)}) %all-to-all-start.7) | async-done | bytes 524320 | tf_op jit(solution)/shard_map/all_to_all | solution.py:55
  378.3 6.9 %all-to-all-start.6 = ((f32[2,128,4,128]{3,2,0,1:T(4,128)}), f32[2,128,4,128]{3,2,0,1:T(4,128)}, u32[]{:S(2)}, u32[]{:S(2)}) async-start(f32[2,128,4,128]{3,2,0,1:T(4,128)} %copy.166), calls=%async_computation.6 | async-start | bytes 1048576 | tf_op jit(solution)/shard_map/all_to_all | solution.py:54
  392.3 9.5 %all-to-all-done.6 = f32[2,128,4,128]{3,2,0,1:T(4,128)} async-done(((f32[2,128,4,128]{3,2,0,1:T(4,128)}), f32[2,128,4,128]{3,2,0,1:T(4,128)}, u32[]{:S(2)}, u32[]{:S(2)}) %all-to-all-start.6) | async-done | bytes 524320 | tf_op jit(solution)/shard_map/all_to_all | solution.py:54
  413.6 10.6 %all-to-all-done.11 = f32[2,128,4,128]{3,2,0,1:T(4,128)S(1)} async-done(((f32[2,128,4,128]{3,2,0,1:T(4,128)}), f32[2,128,4,128]{3,2,0,1:T(4,128)S(1)}, u32[]{:S(2)}, u32[]{:S(2)}) %all-to-all-start.11) | async-done | bytes 524320 | tf_op jit(solution)/shard_map/all_to_all | solution.py:55
  424.2 6.3 %all-to-all-start.10 = ((f32[2,128,4,128]{3,2,0,1:T(4,128)}), f32[2,128,4,128]{3,2,0,1:T(4,128)}, u32[]{:S(2)}, u32[]{:S(2)}) async-start(f32[2,128,4,128]{3,2,0,1:T(4,128)} %copy.190), calls=%async_computation.10 | async-start | bytes 1048576 | tf_op jit(solution)/shard_map/all_to_all | solution.py:54
  435.6 11.7 %all-to-all-done.10 = f32[2,128,4,128]{3,2,0,1:T(4,128)} async-done(((f32[2,128,4,128]{3,2,0,1:T(4,128)}), f32[2,128,4,128]{3,2,0,1:T(4,128)}, u32[]{:S(2)}, u32[]{:S(2)}) %all-to-all-start.10) | async-done | bytes 524320 | tf_op jit(solution)/shard_map/all_to_all | solution.py:54
  447.2 5.8 all-to-all-start.15
  459.2 10.6 %all-to-all-done.15 = f32[2,128,4,128]{3,2,0,1:T(4,128)S(1)} async-done(((f32[2,128,4,128]{3,2,0,1:T(4,128)}), f32[2,128,4,128]{3,2,0,1:T(4,128)S(1)}, u32[]{:S(2)}, u32[]{:S(2)}) %all-to-all-start.15) | async-done | bytes 524320 | tf_op jit(solution)/shard_map/all_to_all | solution.py:55
  469.8 6.3 %all-to-all-start.14 = ((f32[2,128,4,128]{3,2,0,1:T(4,128)}), f32[2,128,4,128]{3,2,0,1:T(4,128)}, u32[]{:S(2)}, u32[]{:S(2)}) async-start(f32[2,128,4,128]{3,2,0,1:T(4,128)} %copy.214), calls=%async_computation.14 | async-start | bytes 1048576 | tf_op jit(solution)/shard_map/all_to_all | solution.py:54
  481.5 11.3 %all-to-all-done.14 = f32[2,128,4,128]{3,2,0,1:T(4,128)} async-done(((f32[2,128,4,128]{3,2,0,1:T(4,128)}), f32[2,128,4,128]{3,2,0,1:T(4,128)}, u32[]{:S(2)}, u32[]{:S(2)}) %all-to-all-start.14) | async-done | bytes 524320 | tf_op jit(solution)/shard_map/all_to_all | solution.py:54
  504.2 71.3 %reduce-scatter.2.cloned.1.call-done = f32[4,4,16,128]{3,2,1,0:T(8,128)} async-done(((f32[4,4,128,128]{3,2,1,0:T(8,128)}), f32[4,4,16,128]{3,2,1,0:T(8,128)}) %reduce-scatter.2.cloned.1.call-update) | async-done | bytes 131088 | tf_op jit(solution)/shard_map/reduce_scatter | solution.py:81
  (171 shorter events, 127.1 us)
Async XLA Ops:
  7.2 104.8 %all-reduce.3.cloned.1.call-start = ((), (), s32[]{:S(2)}) async-start(), calls=%async_computation.18 | async-start | bytes 2097152 | tf_op jit(solution)/shard_map/psum | solution.py:16
  21.3 90.7 %copy-start = (f32[2,4,128,128]{3,2,1,0:T(8,128)S(1)}, f32[2,4,128,128]{3,2,1,0:T(8,128)}, u32[]{:S(2)}) copy-start(f32[2,4,128,128]{3,2,1,0:T(8,128)} %param.3) | copy-start | bytes 1572868
  111.9 1.8 copy-start.6
  111.9 2.7 copy-start.4
  120.0 29.8 %all-to-all-start = ((f32[2,4,128,128]{3,1,0,2:T(4,128)}), f32[2,4,128,128]{3,1,0,2:T(4,128)}, u32[]{:S(2)}, u32[]{:S(2)}) async-start(f32[2,4,128,128]{3,1,0,2:T(4,128)} %copy.129), calls=%async_computation | async-start | bytes 1048576 | tf_op jit(solution)/shard_map/all_to_all | solution.py:44
  140.1 15.5 %copy-start.3 = (f32[4,128,128]{2,1,0:T(8,128)S(1)}, f32[4,128,128]{2,1,0:T(8,128)}, u32[]{:S(2)}) copy-start(f32[4,128,128]{2,1,0:T(8,128)} %get-tuple-element.5) | copy-start | bytes 786436
  149.9 22.5 %all-to-all-start.1 = ((f32[2,4,128,128]{3,1,0,2:T(4,128)}), f32[2,4,128,128]{3,1,0,2:T(4,128)S(1)}, u32[]{:S(2)}, u32[]{:S(2)}) async-start(f32[2,4,128,128]{3,1,0,2:T(4,128)} %copy.134), calls=%async_computation.1 | async-start | bytes 1048576 | tf_op jit(solution)/shard_map/all_to_all | solution.py:45
  156.5 2.5 copy-start.2
  172.4 6.7 %copy-start.20 = (f32[2,4,128,128]{3,1,0,2:T(4,128)}, f32[2,4,128,128]{3,1,0,2:T(4,128)S(1)}, u32[]{:S(2)}) copy-start(f32[2,4,128,128]{3,1,0,2:T(4,128)S(1)} %all-to-all-done.1) | copy-start | bytes 1572868
  172.4 23.2 %all-to-all-start.5 = ((f32[2,4,128,128]{3,1,0,2:T(4,128)}), f32[2,4,128,128]{3,1,0,2:T(4,128)}, u32[]{:S(2)}, u32[]{:S(2)}) async-start(f32[2,4,128,128]{3,1,0,2:T(4,128)} %copy.159), calls=%async_computation.5 | async-start | bytes 1048576 | tf_op jit(solution)/shard_map/all_to_all | solution.py:45
  179.0 1.7 copy-start.17
  183.3 19.5 %copy-start.16 = (f32[2,4,128,128]{3,2,1,0:T(8,128)S(1)}, f32[2,4,128,128]{3,2,1,0:T(8,128)}, u32[]{:S(2)}) copy-start(f32[2,4,128,128]{3,2,1,0:T(8,128)} %fusion.29) | copy-start | bytes 1572868
  195.6 23.1 %all-to-all-start.4 = ((f32[2,4,128,128]{3,1,0,2:T(4,128)}), f32[2,4,128,128]{3,1,0,2:T(4,128)}, u32[]{:S(2)}, u32[]{:S(2)}) async-start(f32[2,4,128,128]{3,1,0,2:T(4,128)} %copy.154), calls=%async_computation.4 | async-start | bytes 1048576 | tf_op jit(solution)/shard_map/all_to_all | solution.py:44
  208.0 2.0 copy-start.5
  208.0 2.0 copy-start.7
  218.7 22.7 %all-to-all-start.9 = ((f32[2,4,128,128]{3,1,0,2:T(4,128)}), f32[2,4,128,128]{3,1,0,2:T(4,128)S(1)}, u32[]{:S(2)}, u32[]{:S(2)}) async-start(f32[2,4,128,128]{3,1,0,2:T(4,128)} %copy.183), calls=%async_computation.9 | async-start | bytes 1048576 | tf_op jit(solution)/shard_map/all_to_all | solution.py:45
  241.4 22.4 %all-to-all-start.8 = ((f32[2,4,128,128]{3,1,0,2:T(4,128)}), f32[2,4,128,128]{3,1,0,2:T(4,128)S(1)}, u32[]{:S(2)}, u32[]{:S(2)}) async-start(f32[2,4,128,128]{3,1,0,2:T(4,128)} %copy.178), calls=%async_computation.8 | async-start | bytes 1048576 | tf_op jit(solution)/shard_map/all_to_all | solution.py:44
  264.7 22.4 %all-to-all-start.13 = ((f32[2,4,128,128]{3,1,0,2:T(4,128)}), f32[2,4,128,128]{3,1,0,2:T(4,128)S(1)}, u32[]{:S(2)}, u32[]{:S(2)}) async-start(f32[2,4,128,128]{3,1,0,2:T(4,128)} %copy.207), calls=%async_computation.13 | async-start | bytes 1048576 | tf_op jit(solution)/shard_map/all_to_all | solution.py:45
  287.0 23.2 %all-to-all-start.12 = ((f32[2,4,128,128]{3,1,0,2:T(4,128)}), f32[2,4,128,128]{3,1,0,2:T(4,128)}, u32[]{:S(2)}, u32[]{:S(2)}) async-start(f32[2,4,128,128]{3,1,0,2:T(4,128)} %copy.202), calls=%async_computation.12 | async-start | bytes 1048576 | tf_op jit(solution)/shard_map/all_to_all | solution.py:44
  310.2 22.4 %all-to-all-start.2 = ((f32[2,128,4,128]{3,2,0,1:T(4,128)}), f32[2,128,4,128]{3,2,0,1:T(4,128)S(1)}, u32[]{:S(2)}, u32[]{:S(2)}) async-start(f32[2,128,4,128]{3,2,0,1:T(4,128)} %copy.142), calls=%async_computation.2 | async-start | bytes 1048576 | tf_op jit(solution)/shard_map/all_to_all | solution.py:54
  332.6 23.2 %all-to-all-start.3 = ((f32[2,128,4,128]{3,2,0,1:T(4,128)}), f32[2,128,4,128]{3,2,0,1:T(4,128)}, u32[]{:S(2)}, u32[]{:S(2)}) async-start(f32[2,128,4,128]{3,2,0,1:T(4,128)} %copy.147), calls=%async_computation.3 | async-start | bytes 1048576 | tf_op jit(solution)/shard_map/all_to_all | solution.py:55
  355.9 22.4 %all-to-all-start.7 = ((f32[2,128,4,128]{3,2,0,1:T(4,128)}), f32[2,128,4,128]{3,2,0,1:T(4,128)S(1)}, u32[]{:S(2)}, u32[]{:S(2)}) async-start(f32[2,128,4,128]{3,2,0,1:T(4,128)} %copy.171), calls=%async_computation.7 | async-start | bytes 1048576 | tf_op jit(solution)/shard_map/all_to_all | solution.py:55
  378.3 23.4 %all-to-all-start.6 = ((f32[2,128,4,128]{3,2,0,1:T(4,128)}), f32[2,128,4,128]{3,2,0,1:T(4,128)}, u32[]{:S(2)}, u32[]{:S(2)}) async-start(f32[2,128,4,128]{3,2,0,1:T(4,128)} %copy.166), calls=%async_computation.6 | async-start | bytes 1048576 | tf_op jit(solution)/shard_map/all_to_all | solution.py:54
  401.8 22.4 %all-to-all-start.11 = ((f32[2,128,4,128]{3,2,0,1:T(4,128)}), f32[2,128,4,128]{3,2,0,1:T(4,128)S(1)}, u32[]{:S(2)}, u32[]{:S(2)}) async-start(f32[2,128,4,128]{3,2,0,1:T(4,128)} %copy.195), calls=%async_computation.11 | async-start | bytes 1048576 | tf_op jit(solution)/shard_map/all_to_all | solution.py:55
  424.2 23.1 %all-to-all-start.10 = ((f32[2,128,4,128]{3,2,0,1:T(4,128)}), f32[2,128,4,128]{3,2,0,1:T(4,128)}, u32[]{:S(2)}, u32[]{:S(2)}) async-start(f32[2,128,4,128]{3,2,0,1:T(4,128)} %copy.190), calls=%async_computation.10 | async-start | bytes 1048576 | tf_op jit(solution)/shard_map/all_to_all | solution.py:54
  447.2 22.5 %all-to-all-start.15 = ((f32[2,128,4,128]{3,2,0,1:T(4,128)}), f32[2,128,4,128]{3,2,0,1:T(4,128)S(1)}, u32[]{:S(2)}, u32[]{:S(2)}) async-start(f32[2,128,4,128]{3,2,0,1:T(4,128)} %copy.219), calls=%async_computation.15 | async-start | bytes 1048576 | tf_op jit(solution)/shard_map/all_to_all | solution.py:55
  469.8 23.1 %all-to-all-start.14 = ((f32[2,128,4,128]{3,2,0,1:T(4,128)}), f32[2,128,4,128]{3,2,0,1:T(4,128)}, u32[]{:S(2)}, u32[]{:S(2)}) async-start(f32[2,128,4,128]{3,2,0,1:T(4,128)} %copy.214), calls=%async_computation.14 | async-start | bytes 1048576 | tf_op jit(solution)/shard_map/all_to_all | solution.py:54
  476.0 99.5 %reduce-scatter.2.cloned.1.call-start = ((), (), s32[]{:S(2)}) async-start(), calls=%async_computation.17 | async-start | bytes 1179648 | tf_op jit(solution)/shard_map/reduce_scatter | solution.py:81
  476.1 1.8 copy-start.11
  478.9 1.7 copy-start.14
  492.8 2.1 copy-start.15
  495.8 1.7 copy-start.9
  (9 other events, 9.7 us)
Sparse Core Ops, SparseCore 0:
  21.4 90.4 all-reduce.2
  503.5 71.9 reduce-scatter.1
where the time goes:
time: 592 us; the launch traced here: 583 us
  waiting for transfers between devices  336 us (57%)
  starting transfers between devices  105 us (18%)
  matrix products  77.6 us (13%)
  local copies, waits for them, and re-layouts  32.5 us (5%)
  between operations  25.6 us (4%)
    psum x1, waiting for transfers between devices, broadcast(): return lax.psum(kept, axis)  89.7 us
    dot_general x80, matrix products, along_axis(): return jnp.einsum(einsum_form, values, matrix, precision=HIGHEST_PRECISION)  77.6 us
    reduce_scatter x1, waiting for transfers between devices, shards(): lax.psum_scatter(partial_sum, 'band', scatter_dimension=2, tiled=True)  71.3 us
    all_to_all x4, waiting for transfers between devices, potentials(): lax.all_to_all(imag_part, 'fft', split_axis=2, concat_axis=1, tiled=True)  51.1 us
    all_to_all x4, waiting for transfers between devices, potentials(): lax.all_to_all(first_part, 'fft', split_axis=1, concat_axis=2, tiled=True)  45.7 us
    all_to_all x4, waiting for transfers between devices, potentials(): lax.all_to_all(second_part, 'fft', split_axis=1, concat_axis=2, tiled=True)  43.9 us
    all_to_all x4, waiting for transfers between devices, potentials(): lax.all_to_all(real_part, 'fft', split_axis=2, concat_axis=1, tiled=True)  34.2 us
    all_to_all x4, starting transfers between devices, potentials(): lax.all_to_all(real_part, 'fft', split_axis=2, concat_axis=1, tiled=True)  32.1 us
  transfers between devices with their start and end apart: 18, of which 18 were waited for; matrix products, arithmetic and copies ran while one was open for 16% of the time, Pallas kernels for 0%

commit v1 on v0

v1 whole, which is shorter than its diff:
```python
import functools

import jax
import jax.numpy as jnp
import ml_dtypes
import numpy as np
from jax import lax
from jax.experimental import pallas as pl
from jax.experimental.pallas import tpu as pltpu
from jax.sharding import PartitionSpec as P

MESH = pl.DeviceIdType.MESH
LEN = 128
COUNT = 4
GROUP = 32
BANDS = 8
PLANES = 4
ROWS = PLANES * LEN


def halves(table):
    high = table.astype(ml_dtypes.bfloat16)
    low = (table - high.astype(np.float64)).astype(ml_dtypes.bfloat16)
    return high, low


def tables():
    n = np.arange(LEN)
    angle = 2.0 * np.pi * ((n[:, None] * n[None, :]) % LEN) / LEN
    cos, sin = np.cos(angle), np.sin(angle)
    forward = np.block([[cos, sin], [-sin, cos]])
    inverse = np.block([[cos, -sin], [sin, cos]])
    natural = np.arange(2 * LEN).reshape(2, GROUP, PLANES)
    rows_y = natural.transpose(1, 0, 2).reshape(-1)
    rows_x = natural.transpose(1, 2, 0).reshape(-1)

    def left(table):
        high, low = halves(table)
        return np.concatenate([high, low, high], axis=1)

    def right(table):
        high, low = halves(table)
        return np.concatenate([high, low, high], axis=0)

    return (
        right(forward.T),
        left(forward[rows_y]),
        left(forward[:, rows_x]),
        left(inverse[rows_x]),
        left(inverse[:, rows_y]),
        right(inverse.T),
    )


def parts(values):
    high = values.astype(jnp.bfloat16)
    low = (values - high.astype(jnp.float32)).astype(jnp.bfloat16)
    return high, low


def apply_left(table, values):
    high, low = parts(values)
    return jnp.dot(table, jnp.concatenate([high, high, low], axis=0), preferred_element_type=jnp.float32)


def apply_right(values, table):
    high, low = parts(values)
    return jnp.dot(jnp.concatenate([high, high, low], axis=1), table, preferred_element_type=jnp.float32)


def kernel(
    owners, orb, kern, fwd_z, fwd_y, fwd_x, inv_x, inv_y, inv_z,
    exch, proj,
    masked, shares, fetched, c_send, c_recv, d_send, d_recv, partial, f_recv,
    s_send, s_recv, g_send, g_recv, cs_sem, cr_sem, ds_sem, dr_sem, fs_sem, fr_sem,
):
    band = lax.axis_index("band")
    pos = lax.axis_index("fft")
    slab = ROWS // BANDS
    block = PLANES * 8
    yrows = LEN // BANDS

    barrier = pltpu.get_barrier_semaphore()

    @pl.loop(1, BANDS)
    def _(k):
        pl.semaphore_signal(barrier, inc=1, device_id={"band": lax.rem(band + k, BANDS)}, device_id_type=MESH)

    @pl.loop(1, GROUP)
    def _(k):
        pl.semaphore_signal(barrier, inc=1, device_id={"fft": lax.rem(pos + k, GROUP)}, device_id_type=MESH)

    for i in range(COUNT):
        first = jnp.where(owners[i] == 2 * band, 1.0, 0.0)
        second = jnp.where(owners[i] == 2 * band + 1, 1.0, 0.0)
        masked[i] = first * orb[0] + second * orb[1]

    exch[...] = jnp.zeros_like(exch)
    pl.semaphore_wait(barrier, BANDS + GROUP - 2)

    def band_copy(src, dst, send, recv, target):
        return pltpu.make_async_remote_copy(
            src_ref=src, dst_ref=dst, send_sem=send, recv_sem=recv, device_id={"band": target}, device_id_type=MESH
        )

    def fft_copy(src, dst, send, recv, target):
        return pltpu.make_async_remote_copy(
            src_ref=src, dst_ref=dst, send_sem=send, recv_sem=recv, device_id={"fft": target}, device_id_type=MESH
        )

    def wait(ref, sem):
        pltpu.make_async_copy(ref, ref, sem).wait()

    mine = pl.ds(pl.multiple_of(band * slab, slab), slab)

    @pl.loop(0, COUNT)
    def _(i):
        @pl.loop(1, BANDS)
        def _(k):
            target = lax.rem(band + k, BANDS)
            theirs = pl.ds(pl.multiple_of(target * slab, slab), slab)
            band_copy(masked.at[i, theirs], shares.at[i, mine], s_send.at[i], s_recv.at[i], target).start()

        shares[i, mine] = masked[i, mine]

    @pl.loop(0, COUNT)
    def _(i):
        wait(shares.at[i, pl.ds(0, slab * (BANDS - 1))], s_recv.at[i])
        total = shares[i, pl.ds(0, slab)]
        for other in range(1, BANDS):
            total += shares[i, pl.ds(other * slab, slab)]
        fetched[i, mine] = total

        @pl.loop(1, BANDS)
        def _(k):
            target = lax.rem(band + k, BANDS)
            band_copy(fetched.at[i, mine], fetched.at[i, mine], g_send.at[i], g_recv.at[i], target).start()

    own = pl.ds(pl.multiple_of(pos * block, block), block)

    def exchange_blocks(send, recv, i, send_sem, recv_sem):
        @pl.loop(1, GROUP)
        def _(k):
            half = (k + 1) // 2
            step = jnp.where(k % 2 == 1, half, GROUP - half)
            target = lax.rem(pos + step, GROUP)
            theirs = pl.ds(pl.multiple_of(target * block, block), block)
            fft_copy(send.at[i, theirs], recv.at[i, own], send_sem.at[i], recv_sem.at[i], target).start()

        recv[i, own] = send[i, own]

    @pl.loop(0, COUNT + 2)
    def _(step):
        @pl.when(step < COUNT)
        def _():
            i = step
            wait(fetched.at[i, pl.ds(0, slab * (BANDS - 1))], g_recv.at[i])
            shared = fetched[i]
            density = jnp.concatenate([shared * orb[0], shared * orb[1]], axis=1)
            lines = apply_right(density, fwd_z[...])
            lines = lines.reshape(PLANES, LEN, 2 * LEN)
            stacked = jnp.concatenate(
                [jnp.concatenate([lines[p, :, :LEN], lines[p, :, LEN:]], axis=0) for p in range(PLANES)], axis=1
            )
            field = apply_left(fwd_y[...], stacked)
            out = jnp.stack([field[:, p * LEN : (p + 1) * LEN].reshape(GROUP, 8, LEN) for p in range(PLANES)], axis=1)
            c_send[i] = out.reshape(GROUP * block, LEN)
            exchange_blocks(c_send, c_recv, i, cs_sem, cr_sem)

        @pl.when((step >= 1) & (step < COUNT + 1))
        def _():
            i = step - 1
            wait(c_recv.at[i, pl.ds(0, block * (GROUP - 1))], cr_sem.at[i])
            columns = jnp.concatenate([c_recv[i, pl.ds(r, 2 * LEN, stride=4), :] for r in range(4)], axis=1)
            modes = apply_left(fwd_x[...], columns)
            scale = jnp.concatenate([kern[pl.ds(r, LEN, stride=4), :] for r in range(4)], axis=1) * (1.0 / LEN**3)
            modes = jnp.concatenate([modes[:LEN] * scale, modes[LEN:] * scale], axis=0)
            back = apply_left(inv_x[...], modes)
            for r in range(4):
                d_send[i, pl.ds(r, 2 * LEN, stride=4), :] = back[:, r * LEN : (r + 1) * LEN]
            exchange_blocks(d_send, d_recv, i, ds_sem, dr_sem)

        @pl.when(step >= 2)
        def _():
            i = step - 2
            wait(d_recv.at[i, pl.ds(0, block * (GROUP - 1))], dr_sem.at[i])
            rows = d_recv[i].reshape(GROUP, PLANES, 8, LEN)
            stacked = jnp.concatenate([rows[:, p].reshape(2 * LEN, LEN) for p in range(PLANES)], axis=1)
            lines = apply_left(inv_y[...], stacked)
            flat = jnp.concatenate(
                [
                    jnp.concatenate(
                        [lines[:LEN, p * LEN : (p + 1) * LEN], lines[LEN:, p * LEN : (p + 1) * LEN]], axis=1
                    )
                    for p in range(PLANES)
                ],
                axis=0,
            )
            field = apply_right(flat, inv_z[...])
            one, two = field[:, :LEN], field[:, LEN:]
            shared = fetched[i]
            exch[0] -= one * shared
            exch[1] -= two * shared
            partial[i] = (-(one * orb[0] + two * orb[1])).reshape(PLANES, LEN, LEN)

            @pl.loop(1, BANDS)
            def _(k):
                target = lax.rem(band + k, BANDS)
                theirs = pl.ds(pl.multiple_of(target * yrows, yrows), yrows)
                band_copy(partial.at[i, :, theirs], f_recv.at[i, band], fs_sem.at[i], fr_sem.at[i], target).start()

            f_recv[i, band] = partial[i, :, pl.ds(pl.multiple_of(band * yrows, yrows), yrows)]

    @pl.loop(0, COUNT)
    def _(i):
        wait(f_recv.at[i, pl.ds(0, BANDS - 1)], fr_sem.at[i])
        total = f_recv[i, 0]
        for other in range(1, BANDS):
            total += f_recv[i, other]
        proj[i] = total

    @pl.loop(0, COUNT)
    def _(i):
        wait(shares.at[i, pl.ds(0, slab * (BANDS - 1))], s_send.at[i])
        wait(fetched.at[i, pl.ds(0, slab * (BANDS - 1))], g_send.at[i])
        wait(c_send.at[i, pl.ds(0, block * (GROUP - 1))], cs_sem.at[i])
        wait(d_send.at[i, pl.ds(0, block * (GROUP - 1))], ds_sem.at[i])
        wait(f_recv.at[i, pl.ds(0, BANDS - 1)], fs_sem.at[i])


def shards(orbitals, owners, weights):
    vmem = pl.BlockSpec(memory_space=pltpu.VMEM)
    smem = pl.BlockSpec(memory_space=pltpu.SMEM)
    wide = pltpu.VMEM((COUNT, GROUP * PLANES * 8, LEN), jnp.float32)
    local = pltpu.VMEM((COUNT, ROWS, LEN), jnp.float32)
    sems = pltpu.SemaphoreType.DMA((COUNT,))
    exchange, projector = pl.pallas_call(
        kernel,
        out_shape=(
            jax.ShapeDtypeStruct((2, ROWS, LEN), jnp.float32),
            jax.ShapeDtypeStruct((COUNT, PLANES, LEN // BANDS, LEN), jnp.float32),
        ),
        in_specs=[smem] + [vmem] * 8,
        out_specs=(vmem, vmem),
        scratch_shapes=[
            local, local, local, wide, wide, wide, wide,
            pltpu.VMEM((COUNT, PLANES, LEN, LEN), jnp.float32),
            pltpu.VMEM((COUNT, BANDS, PLANES, LEN // BANDS, LEN), jnp.float32),
        ]
        + [sems] * 10,
        compiler_params=pltpu.CompilerParams(
            collective_id=0, has_side_effects=True, vmem_limit_bytes=48 * 2**20
        ),
        name="exchange",
    )(
        owners,
        orbitals.reshape(2, ROWS, LEN),
        weights.reshape(LEN * PLANES, LEN),
        *[jnp.asarray(table) for table in tables()],
    )
    return exchange.reshape(2, PLANES, LEN, LEN), projector


def solution(mesh):
    return jax.shard_map(
        shards,
        mesh=mesh,
        in_specs=(P("band", "fft", None, None), P(), P(None, "fft", None)),
        out_specs=(P("band", "fft", None, None), P(None, "fft", "band", None)),
        check_vma=False,
    )
```

time: 592 us -> 141 us (0.24)
  the two profiles are of different devices: /device:TPU:7 before, /device:TPU:25 now
where the time goes in v1:
time: 141 us; the launch traced here: 140 us
  Pallas kernels  129 us (91%)
  local copies, waits for them, and re-layouts  10.1 us (7%)
    pallas_call x1, Pallas kernels, shards(): pl.pallas_call(kernel, out_shape=(jax.ShapeDtypeStruct((2, ROWS, LEN), jn...  129 us
    unnamed x20, local copies, waits for them, and re-layouts  10.1 us

profile of v1, /device:TPU:25, one launch (start us, length us, event | category | flops | bytes accessed | tf_op | source)
XLA Modules:
  0.0 140.1 jit_solution(17612089841131950981)
XLA Ops:
  0.6 0.0 copy-start.8
  0.6 0.6 copy-done.8
  1.3 0.0 copy-start
  1.3 1.0 copy-done
  2.3 0.0 copy-start.1
  2.3 1.0 copy-done.1
  3.3 0.0 copy-start.2
  3.3 1.0 copy-done.2
  4.3 0.0 copy-start.3
  4.3 1.0 copy-done.3
  5.3 0.0 copy-start.4
  5.3 1.0 copy-done.4
  6.3 0.0 copy-start.5
  6.3 1.0 copy-done.5
  7.3 0.0 copy-start.6
  7.3 1.0 copy-done.6
  8.3 0.0 copy-start.7
  8.3 0.9 copy-done.7
  9.3 129.4 %exchange.1 = (f32[2,512,128]{2,1,0:T(8,128)S(1)}, f32[4,4,16,128]{3,2,1,0:T(8,128)S(1)}) custom-call(s32[4]{0:T(128)S(1)} %copy-done.8, f32[2,512,128]{2,1,0:T(8,128)S(1)} %bitcast.4, f32[512,128]{1,0:T(8,128)S(1)} %bitcast.5, bf16[768,256]{1,0:T(8,128)(2,1)S(1)} %copy-done.6, bf16[256,768]{1,0:T(8,128)(2,1)S(1)} %copy-done.5, ...), custom_call_target="tpu_custom_call" | custom-call | tf_op jit(solution)/shard_map/exchange/pallas_call | solution.py:237
  138.6 0.8 copy.13
  139.4 0.7 copy.14
Async XLA Ops:
  0.6 0.7 copy-start.8
  1.3 1.0 copy-start
  2.3 1.0 copy-start.1
  3.3 1.0 copy-start.2
  4.3 1.0 copy-start.3
  5.3 1.0 copy-start.4
  6.3 1.0 copy-start.5
  7.3 1.0 copy-start.6
  8.3 0.9 copy-start.7

commit v2 on v1

--- a/solution.py
+++ b/solution.py
@@ -69,8 +69,9 @@
 
 
 def kernel(
-    owners, orb, kern, fwd_z, fwd_y, fwd_x, inv_x, inv_y, inv_z,
+    owners_in, orb_in, kern_in, fwd_z_in, fwd_y_in, fwd_x_in, inv_x_in, inv_y_in, inv_z_in,
     exch, proj,
+    owners, orb, kern, fwd_z, fwd_y, fwd_x, inv_x, inv_y, inv_z, load_sem,
     masked, shares, fetched, c_send, c_recv, d_send, d_recv, partial, f_recv,
     s_send, s_recv, g_send, g_recv, cs_sem, cr_sem, ds_sem, dr_sem, fs_sem, fr_sem,
 ):
@@ -80,6 +81,15 @@
     block = PLANES * 8
     yrows = LEN // BANDS
 
+    loads = [
+        pltpu.make_async_copy(src, dst, load_sem.at[k])
+        for k, (src, dst) in enumerate(
+            [(owners_in, owners), (orb_in, orb), (fwd_z_in, fwd_z), (fwd_y_in, fwd_y), (fwd_x_in, fwd_x), (kern_in, kern),
+             (inv_x_in, inv_x), (inv_y_in, inv_y), (inv_z_in, inv_z)]
+        )
+    ]
+    for load in loads:
+        load.start()
     barrier = pltpu.get_barrier_semaphore()
 
     @pl.loop(1, BANDS)
@@ -90,6 +100,8 @@
     def _(k):
         pl.semaphore_signal(barrier, inc=1, device_id={"fft": lax.rem(pos + k, GROUP)}, device_id_type=MESH)
 
+    loads[0].wait()
+    loads[1].wait()
     for i in range(COUNT):
         first = jnp.where(owners[i] == 2 * band, 1.0, 0.0)
         second = jnp.where(owners[i] == 2 * band + 1, 1.0, 0.0)
@@ -113,8 +125,7 @@
 
     mine = pl.ds(pl.multiple_of(band * slab, slab), slab)
 
-    @pl.loop(0, COUNT)
-    def _(i):
+    def scatter(i):
         @pl.loop(1, BANDS)
         def _(k):
             target = lax.rem(band + k, BANDS)
@@ -123,8 +134,7 @@
 
         shares[i, mine] = masked[i, mine]
 
-    @pl.loop(0, COUNT)
-    def _(i):
+    def gather(i):
         wait(shares.at[i, pl.ds(0, slab * (BANDS - 1))], s_recv.at[i])
         total = shares[i, pl.ds(0, slab)]
         for other in range(1, BANDS):
@@ -135,6 +145,12 @@
         def _(k):
             target = lax.rem(band + k, BANDS)
             band_copy(fetched.at[i, mine], fetched.at[i, mine], g_send.at[i], g_recv.at[i], target).start()
+
+    scatter(0)
+    gather(0)
+    scatter(1)
+    for load in loads[2:]:
+        load.wait()
 
     own = pl.ds(pl.multiple_of(pos * block, block), block)
 
@@ -166,6 +182,14 @@
             out = jnp.stack([field[:, p * LEN : (p + 1) * LEN].reshape(GROUP, 8, LEN) for p in range(PLANES)], axis=1)
             c_send[i] = out.reshape(GROUP * block, LEN)
             exchange_blocks(c_send, c_recv, i, cs_sem, cr_sem)
+
+            @pl.when(step < COUNT - 1)
+            def _():
+                gather(step + 1)
+
+            @pl.when(step < COUNT - 2)
+            def _():
+                scatter(step + 2)
 
         @pl.when((step >= 1) & (step < COUNT + 1))
         def _():
@@ -230,9 +254,10 @@
 
 def shards(orbitals, owners, weights):
     vmem = pl.BlockSpec(memory_space=pltpu.VMEM)
-    smem = pl.BlockSpec(memory_space=pltpu.SMEM)
     wide = pltpu.VMEM((COUNT, GROUP * PLANES * 8, LEN), jnp.float32)
     local = pltpu.VMEM((COUNT, ROWS, LEN), jnp.float32)
+    tall = pltpu.VMEM((6 * LEN, 2 * LEN), jnp.bfloat16)
+    flat = pltpu.VMEM((2 * LEN, 6 * LEN), jnp.bfloat16)
     sems = pltpu.SemaphoreType.DMA((COUNT,))
     exchange, projector = pl.pallas_call(
         kernel,
@@ -240,16 +265,21 @@
             jax.ShapeDtypeStruct((2, ROWS, LEN), jnp.float32),
             jax.ShapeDtypeStruct((COUNT, PLANES, LEN // BANDS, LEN), jnp.float32),
         ),
-        in_specs=[smem] + [vmem] * 8,
+        in_specs=[pl.BlockSpec(memory_space=pltpu.HBM)] * 9,
         out_specs=(vmem, vmem),
         scratch_shapes=[
+            pltpu.SMEM((COUNT,), jnp.int32),
+            pltpu.VMEM((2, ROWS, LEN), jnp.float32),
+            pltpu.VMEM((ROWS, LEN), jnp.float32),
+            tall, flat, flat, flat, flat, tall,
+            pltpu.SemaphoreType.DMA((9,)),
             local, local, local, wide, wide, wide, wide,
             pltpu.VMEM((COUNT, PLANES, LEN, LEN), jnp.float32),
             pltpu.VMEM((COUNT, BANDS, PLANES, LEN // BANDS, LEN), jnp.float32),
         ]
         + [sems] * 10,
         compiler_params=pltpu.CompilerParams(
-            collective_id=0, has_side_effects=True, vmem_limit_bytes=48 * 2**20
+            collective_id=0, has_side_effects=True, vmem_limit_bytes=64 * 2**20 - 2**16
         ),
         name="exchange",
     )(

time: 141 us -> 128 us (0.908)
  the two profiles are of different devices: /device:TPU:25 before, /device:TPU:24 now
where the time goes in v2:
time: 128 us
  Pallas kernels  125 us (98%)
  local copies, waits for them, and re-layouts  2.57 us (2%)
    pallas_call x1, Pallas kernels, shards(): pl.pallas_call(kernel, out_shape=(jax.ShapeDtypeStruct((2, ROWS, LEN), jn...  125 us
    unnamed x4, local copies, waits for them, and re-layouts  2.57 us

profile of v2, /device:TPU:24, one launch (start us, length us, event | category | flops | bytes accessed | tf_op | source)
XLA Modules:
  0.0 128.3 jit_solution(14778786614007204518)
XLA Ops:
  0.6 125.1 %exchange.1 = (f32[2,512,128]{2,1,0:T(8,128)}, f32[4,4,16,128]{3,2,1,0:T(8,128)}) custom-call(s32[4]{0:T(128)} %owners_in.1, f32[2,512,128]{2,1,0:T(8,128)} %bitcast.4, f32[512,128]{1,0:T(8,128)} %bitcast.5, bf16[768,256]{1,0:T(8,128)(2,1)} %constant.12.clone.fwd_z_in, bf16[256,768]{1,0:T(8,128)(2,1)} %constant.13.clone.fwd_y_in, ...), custom_call_target="tpu_custom_call" | custom-call | tf_op jit(solution)/shard_map/exchange/pallas_call | solution.py:262
  125.7 0.0 copy-start
  125.7 1.9 %copy.13 = f32[2,4,128,128]{3,2,1,0:T(8,128)} copy(f32[2,4,128,128]{3,2,1,0:T(8,128)} %bitcast.3) | data formatting | bytes 1048576
  127.6 0.0 copy-done
  127.6 0.7 copy.14
Async XLA Ops:
  125.7 1.9 %copy-start = (f32[4,4,16,128]{3,2,1,0:T(8,128)S(1)}, f32[4,4,16,128]{3,2,1,0:T(8,128)}, u32[]{:S(2)}) copy-start(f32[4,4,16,128]{3,2,1,0:T(8,128)} %get-tuple-element.9) | copy-start | bytes 393220

commit v3 on v1

v3 whole, which is shorter than its diff:
```python
import functools

import jax
import jax.numpy as jnp
import ml_dtypes
import numpy as np
from jax import lax
from jax.experimental import pallas as pl
from jax.experimental.pallas import tpu as pltpu
from jax.sharding import PartitionSpec as P

MESH = pl.DeviceIdType.MESH
LEN = 128
COUNT = 4
GROUP = 32
BANDS = 8
PLANES = 4
ROWS = PLANES * LEN


def halves(table):
    high = table.astype(ml_dtypes.bfloat16)
    low = (table - high.astype(np.float64)).astype(ml_dtypes.bfloat16)
    return high, low


def tables():
    n = np.arange(LEN)
    angle = 2.0 * np.pi * ((n[:, None] * n[None, :]) % LEN) / LEN
    cos, sin = np.cos(angle), np.sin(angle)
    forward = np.block([[cos, sin], [-sin, cos]])
    inverse = np.block([[cos, -sin], [sin, cos]])
    rows_y = np.arange(2 * LEN).reshape(2, GROUP, PLANES).transpose(1, 0, 2).reshape(-1)
    place, j = np.arange(GROUP)[:, None], np.arange(PLANES)[None, :]
    x, y_hi, y_lo, core = place // 8, place // 4 % 2, place // 2 % 2, place % 2
    plane = 64 * y_lo + 8 * (2 * j + 1 - core) + 4 * y_hi + x
    rows_x = np.stack([plane, plane + LEN], axis=-1).reshape(-1)

    def left(table):
        high, low = halves(table)
        return np.concatenate([high, low, high], axis=1)

    def right(table):
        high, low = halves(table)
        return np.concatenate([high, low, high], axis=0)

    return (
        right(forward.T),
        left(forward[rows_y]),
        left(forward[:, rows_x]),
        left(inverse[rows_x]),
        left(inverse[:, rows_y]),
        right(inverse.T),
    )


def parts(values):
    high = values.astype(jnp.bfloat16)
    low = (values - high.astype(jnp.float32)).astype(jnp.bfloat16)
    return high, low


def apply_left(table, values):
    high, low = parts(values)
    return jnp.dot(table, jnp.concatenate([high, high, low], axis=0), preferred_element_type=jnp.float32)


def apply_right(values, table):
    high, low = parts(values)
    return jnp.dot(jnp.concatenate([high, high, low], axis=1), table, preferred_element_type=jnp.float32)


def kernel(
    owners_in, orb_in, kern_in, fwd_z_in, fwd_y_in, fwd_x_in, inv_x_in, inv_y_in, inv_z_in,
    exch, proj,
    owners, orb, kern_own, fwd_z, fwd_y, fwd_x, inv_x, inv_y, inv_z, load_sem,
    res, inter, chosen, kern, fetched, c_send, c_recv, d_send, d_recv, total, back_recv, partial, f_recv, shared_sum, p_recv, br_sem,
    as_sem, ar_sem, bs_sem, ks_sem, kr_sem, es_sem, er_sem,
    gs_sem, gr_sem, cs_sem, cr_sem, ds_sem, dr_sem, fs_sem, fr_sem, ps_sem, pr_sem,
):
    band = lax.axis_index("band")
    pos = lax.axis_index("fft")
    x, y_hi = band // 2, band % 2
    y_lo, z, core = pos // 16, pos // 2 % 8, pos % 2
    half = LEN // 2
    block = PLANES * 8
    yrows = LEN // BANDS

    def device(to_band, to_y_lo, to_z, to_core):
        return (to_band, 16 * to_y_lo + 2 * to_z + to_core)

    def remote(src, dst, send, recv, target):
        return pltpu.make_async_remote_copy(
            src_ref=src, dst_ref=dst, send_sem=send, recv_sem=recv, device_id=target, device_id_type=MESH
        )

    def wait(ref, sem):
        pltpu.make_async_copy(ref, ref, sem).wait()

    def rows(index, size):
        return pl.ds(pl.multiple_of(index * size, size), size)

    loads = [
        pltpu.make_async_copy(src, dst, load_sem.at[k])
        for k, (src, dst) in enumerate(
            [(orb_in, orb), (owners_in, owners), (kern_in, kern_own), (fwd_z_in, fwd_z), (fwd_y_in, fwd_y),
             (fwd_x_in, fwd_x), (inv_x_in, inv_x), (inv_y_in, inv_y), (inv_z_in, inv_z)]
        )
    ]
    for load in loads:
        load.start()

    place = 4 * band + 2 * y_lo + core
    mine = 16 * y_lo + 2 * ((band - z + 8) % 8) + core

    barrier = pltpu.get_barrier_semaphore()

    def greet(target):
        pl.semaphore_signal(barrier, inc=1, device_id=target, device_id_type=MESH)

    @pl.loop(1, GROUP)
    def _(k):
        other = (place + k) % GROUP
        greet(device(other // 4, other // 2 % 2, z, other % 2))

    @pl.loop(1, 16)
    def _(k):
        other = (2 * z + core + k) % 16
        greet((band, 16 * y_lo + other))

    for load in loads[:3]:
        load.wait()
    total[...] = jnp.zeros_like(total)
    pl.semaphore_wait(barrier, GROUP - 1 + 15)

    mirror = (band - z + 8) % 8

    @pl.when(mirror == z)
    def _():
        pltpu.make_async_copy(kern_own, kern, kr_sem).start()

    @pl.when(mirror != z)
    def _():
        remote(kern_own, kern, ks_sem, kr_sem, device(band, y_lo, mirror, core)).start()

    for step in (2, 1, 3, 0):
        r = (x + step) % PLANES
        for h in range(2):
            src = orb.at[:, rows(2 * r + h, half)]
            dst = inter.at[rows(band, 2)]
            local = (band == 2 * r + core) & (core == h)

            @pl.when(local)
            def _():
                pltpu.make_async_copy(src, dst, br_sem.at[band]).start()

            @pl.when(jnp.logical_not(local))
            def _():
                remote(src, dst, bs_sem, br_sem.at[band], device(2 * r + core, y_lo, z, h)).start()

    def to_planes(odd, src, dst, send, recv):
        target_core = 1 - z % 2
        for step in range(4):
            to = 2 * ((z // 2 + 2 + step) % 4) + odd
            local = (to == z) & (target_core == core)

            @pl.when(local)
            def _():
                pltpu.make_async_copy(src(to), dst, recv).start()

            @pl.when(jnp.logical_not(local))
            def _():
                remote(src(to), dst, send, recv, device(band, y_lo, to, target_core)).start()

    slot = rows(2 * (z // 2) + core, half)

    def select(i):
        chosen[i] = inter[owners[i]]

    def spread(i, odd):
        to_planes(odd, lambda to: chosen.at[i], fetched.at[i, slot], gs_sem.at[i], gr_sem.at[i])

    def arrived(odd):
        for step in range(4):
            source = 2 * step + odd
            wait(inter.at[rows(source, 2)], br_sem.at[source])

    def resident(odd):
        to_planes(odd, lambda to: inter.at[rows(to, 2)], res.at[:, slot], as_sem, ar_sem)

    arrived(0)
    resident(0)
    arrived(1)
    select(0)
    spread(0, 0)
    resident(1)
    spread(0, 1)
    for load in loads[3:]:
        load.wait()

    select(1)
    spread(1, 0)
    spread(1, 1)
    wait(res, ar_sem)

    @pl.loop(0, COUNT + 3)
    def _(step):
        @pl.when(step < COUNT)
        def _():
            i = step
            wait(fetched.at[i], gr_sem.at[i])
            shared = fetched[i]
            density = jnp.concatenate([shared * res[0], shared * res[1]], axis=1)
            lines = apply_right(density, fwd_z[...])
            lines = lines.reshape(PLANES, LEN, 2 * LEN)
            stacked = jnp.concatenate(
                [jnp.concatenate([lines[p, :, :LEN], lines[p, :, LEN:]], axis=0) for p in range(PLANES)], axis=1
            )
            field = apply_left(fwd_y[...], stacked)
            out = jnp.stack([field[:, p * LEN : (p + 1) * LEN].reshape(GROUP, 8, LEN) for p in range(PLANES)], axis=1)
            c_send[i] = out.reshape(GROUP * block, LEN)

            @pl.loop(1, GROUP)
            def _(k):
                other = (mine + 11 * k) % GROUP
                remote(
                    c_send.at[i, rows(other, block)], c_recv.at[i, rows(place, block)], cs_sem.at[i], cr_sem.at[i],
                    device((other // 2 % 8 + z) % 8, other // 16, z, other % 2),
                ).start()

            c_recv[i, rows(place, block)] = c_send[i, rows(mine, block)]

            @pl.when(step < COUNT - 2)
            def _():
                select(step + 2)
                spread(step + 2, 0)
                spread(step + 2, 1)

        @pl.when((step >= 1) & (step < COUNT + 1))
        def _():
            i = step - 1

            @pl.when(i == 0)
            def _():
                wait(kern, kr_sem)

            wait(c_recv.at[i, pl.ds(0, block * (GROUP - 1))], cr_sem.at[i])
            columns = jnp.concatenate([c_recv[i, pl.ds(r, 2 * LEN, stride=4), :] for r in range(4)], axis=1)
            modes = apply_left(fwd_x[...], columns)
            scale = jnp.concatenate([kern[pl.ds(r, LEN, stride=4), :] for r in range(4)], axis=1) * (1.0 / LEN**3)
            modes = jnp.concatenate([modes[:LEN] * scale, modes[LEN:] * scale], axis=0)
            back = apply_left(inv_x[...], modes)
            for r in range(4):
                d_send[i, pl.ds(r, 2 * LEN, stride=4), :] = back[:, r * LEN : (r + 1) * LEN]

            @pl.loop(1, GROUP)
            def _(k):
                other = (place + 11 * k) % GROUP
                remote(
                    d_send.at[i, rows(other, block)], d_recv.at[i, rows(mine, block)], ds_sem.at[i], dr_sem.at[i],
                    device(other // 4, other // 2 % 2, z, other % 2),
                ).start()

            d_recv[i, rows(mine, block)] = d_send[i, rows(place, block)]

        @pl.when((step >= 2) & (step < COUNT + 2))
        def _():
            i = step - 2
            wait(d_recv.at[i, pl.ds(0, block * (GROUP - 1))], dr_sem.at[i])
            tiles = d_recv[i].reshape(GROUP, PLANES, 8, LEN)
            stacked = jnp.concatenate([tiles[:, p].reshape(2 * LEN, LEN) for p in range(PLANES)], axis=1)
            lines = apply_left(inv_y[...], stacked)
            flat = jnp.concatenate(
                [
                    jnp.concatenate(
                        [lines[:LEN, p * LEN : (p + 1) * LEN], lines[LEN:, p * LEN : (p + 1) * LEN]], axis=1
                    )
                    for p in range(PLANES)
                ],
                axis=0,
            )
            field = apply_right(flat, inv_z[...])
            one, two = field[:, :LEN], field[:, LEN:]
            shared = fetched[i]
            total[0] -= one * shared
            total[1] -= two * shared

            @pl.when(i == COUNT - 1)
            def _():
                for step_z in (2, 1, 3, 0):
                    j = (z // 2 + step_z) % PLANES
                    remote(
                        total.at[:, rows(j, LEN)], back_recv.at[:, rows(x, LEN)], es_sem, er_sem,
                        device(z, y_lo, 2 * j + 1 - core, y_hi),
                    ).start()

            partial[i] = -(one * res[0] + two * res[1])

            @pl.loop(0, 2 * PLANES)
            def _(k):
                j, to_core = (z // 2 + 2 + k // 2) % PLANES, k % 2
                to_z = 2 * j + 1 - core
                src = partial.at[i, rows(2 * j + to_core, half)]
                dst = f_recv.at[i, z]
                local = (to_z == z) & (to_core == core)

                @pl.when(local)
                def _():
                    pltpu.make_async_copy(src, dst, fr_sem.at[i]).start()

                @pl.when(jnp.logical_not(local))
                def _():
                    remote(src, dst, fs_sem.at[i], fr_sem.at[i], device(band, y_lo, to_z, to_core)).start()

        @pl.when(step >= 3)
        def _():
            i = step - 3
            wait(f_recv.at[i], fr_sem.at[i])
            summed = f_recv[i, 0]
            for other in range(1, 8):
                summed += f_recv[i, other]
            shared_sum[i] = summed

            @pl.loop(0, 4)
            def _(k):
                to = 4 * core + k
                src = shared_sum.at[i, rows(k, yrows)]
                dst = p_recv.at[i, x]
                local = (to == band) & (y_hi == core)

                @pl.when(local)
                def _():
                    pltpu.make_async_copy(src, dst, pr_sem.at[i]).start()

                @pl.when(jnp.logical_not(local))
                def _():
                    remote(src, dst, ps_sem.at[i], pr_sem.at[i], device(to, y_lo, z, y_hi)).start()

    @pl.loop(0, COUNT)
    def _(i):
        wait(p_recv.at[i], pr_sem.at[i])
        proj[i] = p_recv[i]

    wait(back_recv, er_sem)
    exch[...] = back_recv[...]

    wait(total, es_sem)

    @pl.when(core == y_hi)
    def _():
        wait(inter.at[pl.ds(0, 14)], bs_sem)

    @pl.when(core != y_hi)
    def _():
        wait(inter, bs_sem)

    @pl.when(mirror != z)
    def _():
        wait(kern, ks_sem)

    @pl.when(core == 1 - z % 2)
    def _():
        wait(inter.at[pl.ds(0, 14)], as_sem)

    @pl.when(core == z % 2)
    def _():
        wait(inter, as_sem)

    @pl.loop(0, COUNT)
    def _(i):
        @pl.when(core == 1 - z % 2)
        def _():
            wait(fetched.at[i, pl.ds(0, 7 * half)], gs_sem.at[i])

        @pl.when(core == z % 2)
        def _():
            wait(fetched.at[i], gs_sem.at[i])

        wait(c_send.at[i, pl.ds(0, block * (GROUP - 1))], cs_sem.at[i])
        wait(d_send.at[i, pl.ds(0, block * (GROUP - 1))], ds_sem.at[i])

        @pl.when(core == 1 - z % 2)
        def _():
            wait(partial.at[i, pl.ds(0, ROWS - half)], fs_sem.at[i])

        @pl.when(core == z % 2)
        def _():
            wait(partial.at[i], fs_sem.at[i])

        @pl.when((core == band // 4) & (core == y_hi))
        def _():
            wait(p_recv.at[i, pl.ds(0, 3)], ps_sem.at[i])

        @pl.when((core != band // 4) | (core != y_hi))
        def _():
            wait(p_recv.at[i], ps_sem.at[i])


def shards(orbitals, owners, weights):
    vmem = pl.BlockSpec(memory_space=pltpu.VMEM)
    wide = pltpu.VMEM((COUNT, GROUP * PLANES * 8, LEN), jnp.float32)
    local = pltpu.VMEM((COUNT, ROWS, LEN), jnp.float32)
    pair = pltpu.VMEM((2, ROWS, LEN), jnp.float32)
    single = pltpu.VMEM((ROWS, LEN), jnp.float32)
    tall = pltpu.VMEM((6 * LEN, 2 * LEN), jnp.bfloat16)
    flat = pltpu.VMEM((2 * LEN, 6 * LEN), jnp.bfloat16)
    sem = pltpu.SemaphoreType.DMA
    sems = pltpu.SemaphoreType.DMA((COUNT,))
    exchange, projector = pl.pallas_call(
        kernel,
        out_shape=(
            jax.ShapeDtypeStruct((2, ROWS, LEN), jnp.float32),
            jax.ShapeDtypeStruct((COUNT, PLANES, LEN // BANDS, LEN), jnp.float32),
        ),
        in_specs=[pl.BlockSpec(memory_space=pltpu.HBM)] * 9,
        out_specs=(vmem, vmem),
        scratch_shapes=[
            pltpu.SMEM((COUNT,), jnp.int32), pair, single,
            tall, flat, flat, flat, flat, tall,
            pltpu.SemaphoreType.DMA((9,)),
            pair,
            pltpu.VMEM((2 * BANDS, LEN // 2, LEN), jnp.float32),
            pltpu.VMEM((COUNT, LEN // 2, LEN), jnp.float32),
            single, local, wide, wide, wide, wide, pair, pair, local,
            pltpu.VMEM((COUNT, 8, LEN // 2, LEN), jnp.float32),
            pltpu.VMEM((COUNT, LEN // 2, LEN), jnp.float32),
            pltpu.VMEM((COUNT, PLANES, LEN // BANDS, LEN), jnp.float32),
            pltpu.SemaphoreType.DMA((8,)),
        ]
        + [sem] * 7
        + [sems] * 10,
        compiler_params=pltpu.CompilerParams(
            collective_id=0, has_side_effects=True, vmem_limit_bytes=64 * 2**20 - 2**16
        ),
        name="exchange",
    )(
        owners,
        orbitals.reshape(2, ROWS, LEN),
        weights.reshape(LEN * PLANES, LEN),
        *[jnp.asarray(table) for table in tables()],
    )
    return exchange.reshape(2, PLANES, LEN, LEN), projector


def solution(mesh):
    return jax.shard_map(
        shards,
        mesh=mesh,
        in_specs=(P("band", "fft", None, None), P(), P(None, "fft", None)),
        out_specs=(P("band", "fft", None, None), P(None, "fft", "band", None)),
        check_vma=False,
    )
```

time: 141 us -> 125 us (0.89)
  the two profiles are of different devices: /device:TPU:25 before, /device:TPU:7 now
where the time goes in v3:
time: 125 us; the launch traced here: 123 us
  Pallas kernels  119 us (95%)
  local copies, waits for them, and re-layouts  2.57 us (2%)
    pallas_call x1, Pallas kernels, shards(): pl.pallas_call(kernel, out_shape=(jax.ShapeDtypeStruct((2, ROWS, LEN), jn...  119 us
    unnamed x4, local copies, waits for them, and re-layouts  2.57 us

profile of v3, /device:TPU:7, one launch (start us, length us, event | category | flops | bytes accessed | tf_op | source)
XLA Modules:
  0.0 122.6 jit_solution(14652725958819554415)
XLA Ops:
  0.6 119.4 %exchange.1 = (f32[2,512,128]{2,1,0:T(8,128)}, f32[4,4,16,128]{3,2,1,0:T(8,128)}) custom-call(s32[4]{0:T(128)} %owners_in.1, f32[2,512,128]{2,1,0:T(8,128)} %bitcast.4, f32[512,128]{1,0:T(8,128)} %bitcast.5, bf16[768,256]{1,0:T(8,128)(2,1)} %constant.12.clone.fwd_z_in, bf16[256,768]{1,0:T(8,128)(2,1)} %constant.13.clone.fwd_y_in, ...), custom_call_target="tpu_custom_call" | custom-call | tf_op jit(solution)/shard_map/exchange/pallas_call | solution.py:409
  120.0 0.0 copy-start
  120.0 1.9 %copy.13 = f32[2,4,128,128]{3,2,1,0:T(8,128)} copy(f32[2,4,128,128]{3,2,1,0:T(8,128)} %bitcast.3) | data formatting | bytes 1048576
  121.9 0.0 copy-done
  121.9 0.7 copy.14
Async XLA Ops:
  120.0 1.9 %copy-start = (f32[4,4,16,128]{3,2,1,0:T(8,128)S(1)}, f32[4,4,16,128]{3,2,1,0:T(8,128)}, u32[]{:S(2)}) copy-start(f32[4,4,16,128]{3,2,1,0:T(8,128)} %get-tuple-element.9) | copy-start | bytes 393220

commit v4 on v3

--- a/solution.py
+++ b/solution.py
@@ -14,6 +14,7 @@
 COUNT = 4
 GROUP = 32
 BANDS = 8
+ORDER = ((2, 2), (2, 1), (1, 2), (2, 3), (3, 2), (2, 0), (0, 2), (1, 1), (3, 3), (1, 3), (3, 1), (1, 0), (0, 1), (3, 0), (0, 3), (0, 0))
 PLANES = 4
 ROWS = PLANES * LEN
 
@@ -83,6 +84,7 @@
     x, y_hi = band // 2, band % 2
     y_lo, z, core = pos // 16, pos // 2 % 8, pos % 2
     half = LEN // 2
+    turn = 1 - 2 * core
     block = PLANES * 8
     yrows = LEN // BANDS
 
@@ -118,50 +120,81 @@
     def greet(target):
         pl.semaphore_signal(barrier, inc=1, device_id=target, device_id_type=MESH)
 
-    @pl.loop(1, GROUP)
-    def _(k):
-        other = (place + k) % GROUP
-        greet(device(other // 4, other // 2 % 2, z, other % 2))
+    def wrap(value, size):
+        return jnp.where(value >= size, value - size, value)
+
+    others = []
+    step_by = jnp.where(core == 0, 1, 3)
+    x_at = [x, wrap(x + step_by, 4), wrap(x + 2, 4), wrap(x + 4 - step_by, 4)]
+    y_all = 2 * y_hi + y_lo
+    y_at = []
+    for value in (y_all, wrap(y_all + step_by, 4), wrap(y_all + 2, 4), wrap(y_all + 4 - step_by, 4)):
+        upper = jnp.where(value >= 2, 1, 0)
+        y_at.append((upper, value - 2 * upper))
+    for dx, dy in ORDER:
+        to_band = 2 * x_at[dx] + y_at[dy][0]
+        to_y_lo = y_at[dy][1]
+        to_zeta = wrap(to_band + 8 - z, 8)
+        for flip in range(2):
+            if (dx, dy, flip) != (0, 0, 0):
+                to_core = core if flip == 0 else 1 - core
+                others.append((
+                    (to_band, 16 * to_y_lo + 2 * z + to_core),
+                    4 * to_band + 2 * to_y_lo + to_core,
+                    16 * to_y_lo + 2 * to_zeta + to_core,
+                ))
+
+    for target, _, _ in others:
+        greet(target)
 
     @pl.loop(1, 16)
     def _(k):
         other = (2 * z + core + k) % 16
         greet((band, 16 * y_lo + other))
 
+    greet(device((band + 4) % BANDS, y_lo, (band - z + 8) % 8, core))
     for load in loads[:3]:
         load.wait()
     total[...] = jnp.zeros_like(total)
-    pl.semaphore_wait(barrier, GROUP - 1 + 15)
+    pl.semaphore_wait(barrier, GROUP - 1 + 15 + 1)
 
     mirror = (band - z + 8) % 8
+    across = (band + 4) % BANDS
+    near, far = pl.ds(0, ROWS // 2), pl.ds(ROWS // 2, ROWS // 2)
+    remote(
+        kern_own.at[far], kern.at[far], ks_sem.at[1], kr_sem.at[1], device(across, y_lo, (across - z + 8) % 8, core)
+    ).start()
 
     @pl.when(mirror == z)
     def _():
-        pltpu.make_async_copy(kern_own, kern, kr_sem).start()
+        pltpu.make_async_copy(kern_own.at[near], kern.at[near], kr_sem.at[0]).start()
 
     @pl.when(mirror != z)
     def _():
-        remote(kern_own, kern, ks_sem, kr_sem, device(band, y_lo, mirror, core)).start()
-
-    for step in (2, 1, 3, 0):
-        r = (x + step) % PLANES
-        for h in range(2):
-            src = orb.at[:, rows(2 * r + h, half)]
-            dst = inter.at[rows(band, 2)]
-            local = (band == 2 * r + core) & (core == h)
-
-            @pl.when(local)
-            def _():
-                pltpu.make_async_copy(src, dst, br_sem.at[band]).start()
-
-            @pl.when(jnp.logical_not(local))
-            def _():
-                remote(src, dst, bs_sem, br_sem.at[band], device(2 * r + core, y_lo, z, h)).start()
+        remote(
+            kern_own.at[near], kern.at[near], ks_sem.at[0], kr_sem.at[0], device(band, y_lo, mirror, core)
+        ).start()
+
+    for a in range(2):
+        for step in (2, 1, 3, 0):
+            r = (x + turn * step + PLANES) % PLANES
+            for h in range(2):
+                src = orb.at[a, rows(2 * r + h, half)]
+                dst = inter.at[2 * band + a]
+                local = (band == 2 * r + core) & (core == h)
+
+                @pl.when(local)
+                def _():
+                    pltpu.make_async_copy(src, dst, br_sem.at[a, band]).start()
+
+                @pl.when(jnp.logical_not(local))
+                def _():
+                    remote(src, dst, bs_sem, br_sem.at[a, band], device(2 * r + core, y_lo, z, h)).start()
 
     def to_planes(odd, src, dst, send, recv):
         target_core = 1 - z % 2
         for step in range(4):
-            to = 2 * ((z // 2 + 2 + step) % 4) + odd
+            to = 2 * ((z // 2 + 6 + turn * step) % 4) + odd
             local = (to == z) & (target_core == core)
 
             @pl.when(local)
@@ -180,20 +213,24 @@
     def spread(i, odd):
         to_planes(odd, lambda to: chosen.at[i], fetched.at[i, slot], gs_sem.at[i], gr_sem.at[i])
 
-    def arrived(odd):
+    def arrived(odd, a):
         for step in range(4):
             source = 2 * step + odd
-            wait(inter.at[rows(source, 2)], br_sem.at[source])
-
-    def resident(odd):
-        to_planes(odd, lambda to: inter.at[rows(to, 2)], res.at[:, slot], as_sem, ar_sem)
-
-    arrived(0)
-    resident(0)
-    arrived(1)
+            wait(inter.at[2 * source + a], br_sem.at[a, source])
+
+    def resident(odd, a):
+        to_planes(odd, lambda to: inter.at[2 * to + a], res.at[a, slot], as_sem, ar_sem)
+
+    arrived(0, 0)
+    resident(0, 0)
+    arrived(0, 1)
+    resident(0, 1)
+    arrived(1, 0)
+    arrived(1, 1)
     select(0)
     spread(0, 0)
-    resident(1)
+    resident(1, 0)
+    resident(1, 1)
     spread(0, 1)
     for load in loads[3:]:
         load.wait()
@@ -220,12 +257,10 @@
             out = jnp.stack([field[:, p * LEN : (p + 1) * LEN].reshape(GROUP, 8, LEN) for p in range(PLANES)], axis=1)
             c_send[i] = out.reshape(GROUP * block, LEN)
 
-            @pl.loop(1, GROUP)
-            def _(k):
-                other = (mine + 11 * k) % GROUP
+            for target, _, theirs in others:
                 remote(
-                    c_send.at[i, rows(other, block)], c_recv.at[i, rows(place, block)], cs_sem.at[i], cr_sem.at[i],
-                    device((other // 2 % 8 + z) % 8, other // 16, z, other % 2),
+                    c_send.at[i, rows(theirs, block)], c_recv.at[i, rows(place, block)],
+                    cs_sem.at[i], cr_sem.at[i], target,
                 ).start()
 
             c_recv[i, rows(place, block)] = c_send[i, rows(mine, block)]
@@ -242,7 +277,8 @@
 
             @pl.when(i == 0)
             def _():
-                wait(kern, kr_sem)
+                wait(kern.at[near], kr_sem.at[0])
+                wait(kern.at[far], kr_sem.at[1])
 
             wait(c_recv.at[i, pl.ds(0, block * (GROUP - 1))], cr_sem.at[i])
             columns = jnp.concatenate([c_recv[i, pl.ds(r, 2 * LEN, stride=4), :] for r in range(4)], axis=1)
@@ -253,12 +289,10 @@
             for r in range(4):
                 d_send[i, pl.ds(r, 2 * LEN, stride=4), :] = back[:, r * LEN : (r + 1) * LEN]
 
-            @pl.loop(1, GROUP)
-            def _(k):
-                other = (place + 11 * k) % GROUP
+            for target, theirs, _ in others:
                 remote(
-                    d_send.at[i, rows(other, block)], d_recv.at[i, rows(mine, block)], ds_sem.at[i], dr_sem.at[i],
-                    device(other // 4, other // 2 % 2, z, other % 2),
+                    d_send.at[i, rows(theirs, block)], d_recv.at[i, rows(mine, block)],
+                    ds_sem.at[i], dr_sem.at[i], target,
                 ).start()
 
             d_recv[i, rows(mine, block)] = d_send[i, rows(place, block)]
@@ -282,23 +316,11 @@
             field = apply_right(flat, inv_z[...])
             one, two = field[:, :LEN], field[:, LEN:]
             shared = fetched[i]
-            total[0] -= one * shared
-            total[1] -= two * shared
-
-            @pl.when(i == COUNT - 1)
-            def _():
-                for step_z in (2, 1, 3, 0):
-                    j = (z // 2 + step_z) % PLANES
-                    remote(
-                        total.at[:, rows(j, LEN)], back_recv.at[:, rows(x, LEN)], es_sem, er_sem,
-                        device(z, y_lo, 2 * j + 1 - core, y_hi),
-                    ).start()
-
-            partial[i] = -(one * res[0] + two * res[1])
+            partial[i] = one * res[0] + two * res[1]
 
             @pl.loop(0, 2 * PLANES)
             def _(k):
-                j, to_core = (z // 2 + 2 + k // 2) % PLANES, k % 2
+                j, to_core = (z // 2 + 6 + turn * (k // 2)) % PLANES, k % 2
                 to_z = 2 * j + 1 - core
                 src = partial.at[i, rows(2 * j + to_core, half)]
                 dst = f_recv.at[i, z]
@@ -311,6 +333,19 @@
                 @pl.when(jnp.logical_not(local))
                 def _():
                     remote(src, dst, fs_sem.at[i], fr_sem.at[i], device(band, y_lo, to_z, to_core)).start()
+
+            total[0] += one * shared
+            total[1] += two * shared
+
+            @pl.when(i == COUNT - 1)
+            def _():
+                for step_z in (2, 1, 3, 0):
+                    j = (z // 2 + turn * step_z + PLANES) % PLANES
+                    for a in range(2):
+                        remote(
+                            total.at[a, rows(j, LEN)], back_recv.at[a, rows(x, LEN)], es_sem, er_sem,
+                            device(z, y_lo, 2 * j + 1 - core, y_hi),
+                        ).start()
 
         @pl.when(step >= 3)
         def _():
@@ -354,9 +389,11 @@
     def _():
         wait(inter, bs_sem)
 
+    wait(kern.at[far], ks_sem.at[1])
+
     @pl.when(mirror != z)
     def _():
-        wait(kern, ks_sem)
+        wait(kern.at[near], ks_sem.at[0])
 
     @pl.when(core == 1 - z % 2)
     def _():
@@ -425,9 +462,9 @@
             pltpu.VMEM((COUNT, 8, LEN // 2, LEN), jnp.float32),
             pltpu.VMEM((COUNT, LEN // 2, LEN), jnp.float32),
             pltpu.VMEM((COUNT, PLANES, LEN // BANDS, LEN), jnp.float32),
-            pltpu.SemaphoreType.DMA((8,)),
+            pltpu.SemaphoreType.DMA((2, 8)),
+            sem, sem, sem, sem((2,)), sem((2,)), sem, sem,
         ]
-        + [sem] * 7
         + [sems] * 10,
         compiler_params=pltpu.CompilerParams(
             collective_id=0, has_side_effects=True, vmem_limit_bytes=64 * 2**20 - 2**16
@@ -439,7 +476,7 @@
         weights.reshape(LEN * PLANES, LEN),
         *[jnp.asarray(table) for table in tables()],
     )
-    return exchange.reshape(2, PLANES, LEN, LEN), projector
+    return -exchange.reshape(2, PLANES, LEN, LEN), -projector
 
 
 def solution(mesh):

time: 125 us -> 116 us (0.928); the launches traced: 123 us -> 116 us
  Pallas kernels: 119 us -> 112 us
  other arithmetic: 0 us -> 2.57 us
  local copies, waits for them, and re-layouts: 2.57 us -> 0.01 us
    pallas_call x1, Pallas kernels: 119 us -> 112 us  [shards(): pl.pallas_call(kernel, out_shape=(jax.ShapeDtypeStruct((2, ROWS, LEN), jn...]
    neg x0 -> x2, other arithmetic: none -> 2.57 us  [shards(): return (-exchange.reshape(2, PLANES, LEN, LEN), -projector)]
    unnamed x4 -> x2, local copies, waits for them, and re-layouts: 2.57 us -> 0.01 us
where the time goes in v4:
time: 116 us
  Pallas kernels  112 us (97%)
  other arithmetic  2.57 us (2%)
    pallas_call x1, Pallas kernels, shards(): pl.pallas_call(kernel, out_shape=(jax.ShapeDtypeStruct((2, ROWS, LEN), jn...  112 us
    neg x2, other arithmetic, shards(): return (-exchange.reshape(2, PLANES, LEN, LEN), -projector)  2.57 us

profile of v4, /device:TPU:7, one launch (start us, length us, event | category | flops | bytes accessed | tf_op | source)
XLA Modules:
  0.0 115.7 jit_solution(11909898601020746972)
XLA Ops:
  0.6 112.5 %exchange.1 = (f32[2,512,128]{2,1,0:T(8,128)}, f32[4,4,16,128]{3,2,1,0:T(8,128)}) custom-call(s32[4]{0:T(128)} %owners_in.1, f32[2,512,128]{2,1,0:T(8,128)} %bitcast.4, f32[512,128]{1,0:T(8,128)} %bitcast.5, bf16[768,256]{1,0:T(8,128)(2,1)} %constant.12.clone.fwd_z_in, bf16[256,768]{1,0:T(8,128)(2,1)} %constant.13.clone.fwd_y_in, ...), custom_call_target="tpu_custom_call" | custom-call | tf_op jit(solution)/shard_map/exchange/pallas_call | solution.py:446
  113.1 0.0 copy-start
  113.1 1.9 %neg.9 = f32[2,512,128]{2,1,0:T(8,128)} negate(f32[2,512,128]{2,1,0:T(8,128)} %get-tuple-element.4) | non-fusion elementwise | flops 131072 | bytes 1048576 | tf_op jit(solution)/shard_map/neg | solution.py:479
  115.0 0.0 copy-done
  115.0 0.7 neg.11
Async XLA Ops:
  113.1 1.9 %copy-start = (f32[4,4,16,128]{3,2,1,0:T(8,128)S(1)}, f32[4,4,16,128]{3,2,1,0:T(8,128)}, u32[]{:S(2)}) copy-start(f32[4,4,16,128]{3,2,1,0:T(8,128)} %get-tuple-element.5) | copy-start | bytes 393220

commit v5 on v4

--- a/solution.py
+++ b/solution.py
@@ -75,7 +75,7 @@
     owners_in, orb_in, kern_in, fwd_z_in, fwd_y_in, fwd_x_in, inv_x_in, inv_y_in, inv_z_in,
     exch, proj,
     owners, orb, kern_own, fwd_z, fwd_y, fwd_x, inv_x, inv_y, inv_z, load_sem,
-    res, inter, chosen, kern, fetched, c_send, c_recv, d_send, d_recv, total, back_recv, partial, f_recv, shared_sum, p_recv, br_sem,
+    res, inter, chosen, kern, fetched, c_send, c_recv, d_send, d_recv, total, partial, f_recv, shared_sum, br_sem,
     as_sem, ar_sem, bs_sem, ks_sem, kr_sem, es_sem, er_sem,
     gs_sem, gr_sem, cs_sem, cr_sem, ds_sem, dr_sem, fs_sem, fr_sem, ps_sem, pr_sem,
 ):
@@ -84,7 +84,6 @@
     x, y_hi = band // 2, band % 2
     y_lo, z, core = pos // 16, pos // 2 % 8, pos % 2
     half = LEN // 2
-    turn = 1 - 2 * core
     block = PLANES * 8
     yrows = LEN // BANDS
 
@@ -101,6 +100,15 @@
 
     def rows(index, size):
         return pl.ds(pl.multiple_of(index * size, size), size)
+
+    def either(here, src, dst, recv, far_copy):
+        @pl.when(here)
+        def _():
+            pltpu.make_async_copy(src, dst, recv).start()
+
+        @pl.when(jnp.logical_not(here))
+        def _():
+            far_copy.start()
 
     loads = [
         pltpu.make_async_copy(src, dst, load_sem.at[k])
@@ -126,6 +134,9 @@
     others = []
     step_by = jnp.where(core == 0, 1, 3)
     x_at = [x, wrap(x + step_by, 4), wrap(x + 2, 4), wrap(x + 4 - step_by, 4)]
+    z_half = z // 2
+    z_odd = z - 2 * z_half
+    z_at = [wrap(z_half + 2, 4), wrap(z_half + 4 - step_by, 4), z_half, wrap(z_half + step_by, 4)]
     y_all = 2 * y_hi + y_lo
     y_at = []
     for value in (y_all, wrap(y_all + step_by, 4), wrap(y_all + 2, 4), wrap(y_all + 4 - step_by, 4)):
@@ -158,6 +169,17 @@
     total[...] = jnp.zeros_like(total)
     pl.semaphore_wait(barrier, GROUP - 1 + 15 + 1)
 
+    for a in range(2):
+        for n in (2, 1, 3, 0):
+            for h in range(2):
+                src = orb.at[a, rows(2 * x_at[n] + h, half)]
+                dst = inter.at[2 * band + a]
+                far_copy = remote(src, dst, bs_sem, br_sem.at[a, band], device(2 * x_at[n] + core, y_lo, z, h))
+                if n > 0:
+                    far_copy.start()
+                else:
+                    either((y_hi == core) & (core == h), src, dst, br_sem.at[a, band], far_copy)
+
     mirror = (band - z + 8) % 8
     across = (band + 4) % BANDS
     near, far = pl.ds(0, ROWS // 2), pl.ds(ROWS // 2, ROWS // 2)
@@ -175,37 +197,17 @@
             kern_own.at[near], kern.at[near], ks_sem.at[0], kr_sem.at[0], device(band, y_lo, mirror, core)
         ).start()
 
-    for a in range(2):
-        for step in (2, 1, 3, 0):
-            r = (x + turn * step + PLANES) % PLANES
-            for h in range(2):
-                src = orb.at[a, rows(2 * r + h, half)]
-                dst = inter.at[2 * band + a]
-                local = (band == 2 * r + core) & (core == h)
-
-                @pl.when(local)
-                def _():
-                    pltpu.make_async_copy(src, dst, br_sem.at[a, band]).start()
-
-                @pl.when(jnp.logical_not(local))
-                def _():
-                    remote(src, dst, bs_sem, br_sem.at[a, band], device(2 * r + core, y_lo, z, h)).start()
-
     def to_planes(odd, src, dst, send, recv):
-        target_core = 1 - z % 2
-        for step in range(4):
-            to = 2 * ((z // 2 + 6 + turn * step) % 4) + odd
-            local = (to == z) & (target_core == core)
-
-            @pl.when(local)
-            def _():
-                pltpu.make_async_copy(src(to), dst, recv).start()
-
-            @pl.when(jnp.logical_not(local))
-            def _():
-                remote(src(to), dst, send, recv, device(band, y_lo, to, target_core)).start()
-
-    slot = rows(2 * (z // 2) + core, half)
+        target_core = 1 - z_odd
+        for n in range(4):
+            to = 2 * z_at[n] + odd
+            far_copy = remote(src(to), dst, send, recv, device(band, y_lo, to, target_core))
+            if n != 2:
+                far_copy.start()
+            else:
+                either((z_odd == odd) & (target_core == core), src(to), dst, recv, far_copy)
+
+    slot = rows(2 * z_half + core, half)
 
     def select(i):
         chosen[i] = inter[owners[i]]
@@ -318,32 +320,26 @@
             shared = fetched[i]
             partial[i] = one * res[0] + two * res[1]
 
-            @pl.loop(0, 2 * PLANES)
-            def _(k):
-                j, to_core = (z // 2 + 6 + turn * (k // 2)) % PLANES, k % 2
-                to_z = 2 * j + 1 - core
-                src = partial.at[i, rows(2 * j + to_core, half)]
-                dst = f_recv.at[i, z]
-                local = (to_z == z) & (to_core == core)
-
-                @pl.when(local)
-                def _():
-                    pltpu.make_async_copy(src, dst, fr_sem.at[i]).start()
-
-                @pl.when(jnp.logical_not(local))
-                def _():
-                    remote(src, dst, fs_sem.at[i], fr_sem.at[i], device(band, y_lo, to_z, to_core)).start()
+            for n in range(4):
+                to_z = 2 * z_at[n] + 1 - core
+                for to_core in range(2):
+                    src = partial.at[i, rows(2 * z_at[n] + to_core, half)]
+                    dst = f_recv.at[i, z]
+                    far_copy = remote(src, dst, fs_sem.at[i], fr_sem.at[i], device(band, y_lo, to_z, to_core))
+                    if n != 2:
+                        far_copy.start()
+                    else:
+                        either((z_odd == 1 - core) & (core == to_core), src, dst, fr_sem.at[i], far_copy)
 
             total[0] += one * shared
             total[1] += two * shared
 
             @pl.when(i == COUNT - 1)
             def _():
-                for step_z in (2, 1, 3, 0):
-                    j = (z // 2 + turn * step_z + PLANES) % PLANES
+                for j in z_at:
                     for a in range(2):
                         remote(
-                            total.at[a, rows(j, LEN)], back_recv.at[a, rows(x, LEN)], es_sem, er_sem,
+                            total.at[a, rows(j, LEN)], exch.at[a, rows(x, LEN)], es_sem, er_sem,
                             device(z, y_lo, 2 * j + 1 - core, y_hi),
                         ).start()
 
@@ -356,28 +352,24 @@
                 summed += f_recv[i, other]
             shared_sum[i] = summed
 
-            @pl.loop(0, 4)
-            def _(k):
-                to = 4 * core + k
-                src = shared_sum.at[i, rows(k, yrows)]
-                dst = p_recv.at[i, x]
-                local = (to == band) & (y_hi == core)
-
-                @pl.when(local)
-                def _():
-                    pltpu.make_async_copy(src, dst, pr_sem.at[i]).start()
-
-                @pl.when(jnp.logical_not(local))
-                def _():
-                    remote(src, dst, ps_sem.at[i], pr_sem.at[i], device(to, y_lo, z, y_hi)).start()
+            quarter = band % 4
+            for k in range(4):
+                part = wrap(quarter + k, 4)
+                src = shared_sum.at[i, rows(part, yrows)]
+                dst = proj.at[i, x]
+                far_copy = remote(
+                    src, dst, ps_sem.at[i], pr_sem.at[i], device(4 * core + part, y_lo, z, y_hi)
+                )
+                if k > 0:
+                    far_copy.start()
+                else:
+                    either((band // 4 == core) & (y_hi == core), src, dst, pr_sem.at[i], far_copy)
 
     @pl.loop(0, COUNT)
     def _(i):
-        wait(p_recv.at[i], pr_sem.at[i])
-        proj[i] = p_recv[i]
-
-    wait(back_recv, er_sem)
-    exch[...] = back_recv[...]
+        wait(proj.at[i], pr_sem.at[i])
+
+    wait(exch, er_sem)
 
     wait(total, es_sem)
 
@@ -426,11 +418,16 @@
 
         @pl.when((core == band // 4) & (core == y_hi))
         def _():
-            wait(p_recv.at[i, pl.ds(0, 3)], ps_sem.at[i])
+            wait(proj.at[i, pl.ds(0, 3)], ps_sem.at[i])
 
         @pl.when((core != band // 4) | (core != y_hi))
         def _():
-            wait(p_recv.at[i], ps_sem.at[i])
+            wait(proj.at[i], ps_sem.at[i])
+
+
+def negate(exchange, projector, exchange_out, projector_out):
+    exchange_out[...] = -exchange[...]
+    projector_out[...] = -projector[...]
 
 
 def shards(orbitals, owners, weights):
@@ -450,7 +447,7 @@
             jax.ShapeDtypeStruct((COUNT, PLANES, LEN // BANDS, LEN), jnp.float32),
         ),
         in_specs=[pl.BlockSpec(memory_space=pltpu.HBM)] * 9,
-        out_specs=(vmem, vmem),
+        out_specs=(pl.BlockSpec(memory_space=pltpu.HBM),) * 2,
         scratch_shapes=[
             pltpu.SMEM((COUNT,), jnp.int32), pair, single,
             tall, flat, flat, flat, flat, tall,
@@ -458,10 +455,9 @@
             pair,
             pltpu.VMEM((2 * BANDS, LEN // 2, LEN), jnp.float32),
             pltpu.VMEM((COUNT, LEN // 2, LEN), jnp.float32),
-            single, local, wide, wide, wide, wide, pair, pair, local,
+            single, local, wide, wide, wide, wide, pair, local,
             pltpu.VMEM((COUNT, 8, LEN // 2, LEN), jnp.float32),
             pltpu.VMEM((COUNT, LEN // 2, LEN), jnp.float32),
-            pltpu.VMEM((COUNT, PLANES, LEN // BANDS, LEN), jnp.float32),
             pltpu.SemaphoreType.DMA((2, 8)),
             sem, sem, sem, sem((2,)), sem((2,)), sem, sem,
         ]
@@ -476,7 +472,17 @@
         weights.reshape(LEN * PLANES, LEN),
         *[jnp.asarray(table) for table in tables()],
     )
-    return -exchange.reshape(2, PLANES, LEN, LEN), -projector
+    exchange, projector = pl.pallas_call(
+        negate,
+        out_shape=(
+            jax.ShapeDtypeStruct((2, ROWS, LEN), jnp.float32),
+            jax.ShapeDtypeStruct((COUNT, PLANES, LEN // BANDS, LEN), jnp.float32),
+        ),
+        in_specs=[vmem, vmem],
+        out_specs=(vmem, vmem),
+        name="negate",
+    )(exchange, projector)
+    return exchange.reshape(2, PLANES, LEN, LEN), projector
 
 
 def solution(mesh):

time: 116 us -> 114 us (0.983)
  other arithmetic: 2.57 us -> 0 us
    neg x2 -> x0, other arithmetic: 2.57 us -> none  [shards(): return (-exchange.reshape(2, PLANES, LEN, LEN), -projector)]
    pallas_call x1, Pallas kernels: 112 us -> 110 us  [shards(): pl.pallas_call(kernel, out_shape=(jax.ShapeDtypeStruct((2, ROWS, LEN), jn...]
    pallas_call x0 -> x1, Pallas kernels: none -> 1.93 us  [shards(): pl.pallas_call(negate, out_shape=(jax.ShapeDtypeStruct((2, ROWS, LEN), jn...]
where the time goes in v5:
time: 114 us; the launch traced here: 113 us
  Pallas kernels  112 us (98%)
    pallas_call x1, Pallas kernels, shards(): pl.pallas_call(kernel, out_shape=(jax.ShapeDtypeStruct((2, ROWS, LEN), jn...  110 us

profile of v5, /device:TPU:7, one launch (start us, length us, event | category | flops | bytes accessed | tf_op | source)
XLA Modules:
  0.0 113.0 jit_solution(4811429172465058332)
XLA Ops:
  0.6 110.4 %exchange.1 = (f32[2,512,128]{2,1,0:T(8,128)}, f32[4,4,16,128]{3,2,1,0:T(8,128)}) custom-call(s32[4]{0:T(128)} %owners_in.1, f32[2,512,128]{2,1,0:T(8,128)} %bitcast.3, f32[512,128]{1,0:T(8,128)} %bitcast.4, bf16[768,256]{1,0:T(8,128)(2,1)} %constant.12.clone.fwd_z_in, bf16[256,768]{1,0:T(8,128)(2,1)} %constant.13.clone.fwd_y_in, ...), custom_call_target="tpu_custom_call" | custom-call | tf_op jit(solution)/shard_map/exchange/pallas_call | solution.py:443
  111.0 1.9 %negate.1 = (f32[2,512,128]{2,1,0:T(8,128)}, f32[4,4,16,128]{3,2,1,0:T(8,128)}) custom-call(f32[2,512,128]{2,1,0:T(8,128)} %get-tuple-element.6.exchange, f32[4,4,16,128]{3,2,1,0:T(8,128)} %get-tuple-element.7.projector), custom_call_target="tpu_custom_call" | custom-call | tf_op jit(solution)/shard_map/negate/pallas_call | solution.py:475

commit v6 on v5

--- a/solution.py
+++ b/solution.py
@@ -77,7 +77,7 @@
     owners, orb, kern_own, fwd_z, fwd_y, fwd_x, inv_x, inv_y, inv_z, load_sem,
     res, inter, chosen, kern, fetched, c_send, c_recv, d_send, d_recv, total, partial, f_recv, shared_sum, br_sem,
     as_sem, ar_sem, bs_sem, ks_sem, kr_sem, es_sem, er_sem,
-    gs_sem, gr_sem, cs_sem, cr_sem, ds_sem, dr_sem, fs_sem, fr_sem, ps_sem, pr_sem,
+    gs_sem, gr_sem, gq_sem, cs_sem, cr_sem, ds_sem, dr_sem, fs_sem, fr_sem, ps_sem, pr_sem,
 ):
     band = lax.axis_index("band")
     pos = lax.axis_index("fft")
@@ -212,8 +212,40 @@
     def select(i):
         chosen[i] = inter[owners[i]]
 
-    def spread(i, odd):
-        to_planes(odd, lambda to: chosen.at[i], fetched.at[i, slot], gs_sem.at[i], gr_sem.at[i])
+    relays = core == 1 - z_odd
+
+    def spread(i):
+        dst = fetched.at[i, slot]
+        for step in (2, 6, 1, 7, 0):
+            to = wrap(z + step, 8)
+            recv = gq_sem.at[i] if step in (2, 6) else gr_sem.at[i]
+            far_copy = remote(chosen.at[i], dst, gs_sem.at[i], recv, device(band, y_lo, to, 1 - z_odd))
+            if step > 0:
+                far_copy.start()
+            else:
+                either(relays, chosen.at[i], dst, recv, far_copy)
+
+    def hand_on(i):
+        @pl.when(relays)
+        def _():
+            wait(fetched.at[i, pl.ds(0, 4 * half)], gq_sem.at[i])
+            for source, once, twice, kept in ((6, 1, 2, 0), (2, 7, 6, 1)):
+                from_half = wrap(z + source, 8) // 2
+                for h in (kept, 1 - kept):
+                    held = fetched.at[i, rows(2 * from_half + h, half)]
+                    for step in ((twice, once) if h == kept else (once,)):
+                        remote(
+                            held, held, gs_sem.at[i], gr_sem.at[i], device(band, y_lo, wrap(z + step, 8), core)
+                        ).start()
+
+    def fetched_here(i):
+        @pl.when(relays)
+        def _():
+            wait(fetched.at[i, pl.ds(0, 4 * half)], gr_sem.at[i])
+
+        @pl.when(jnp.logical_not(relays))
+        def _():
+            wait(fetched.at[i], gr_sem.at[i])
 
     def arrived(odd, a):
         for step in range(4):
@@ -230,16 +262,15 @@
     arrived(1, 0)
     arrived(1, 1)
     select(0)
-    spread(0, 0)
+    spread(0)
     resident(1, 0)
     resident(1, 1)
-    spread(0, 1)
     for load in loads[3:]:
         load.wait()
 
+    hand_on(0)
     select(1)
-    spread(1, 0)
-    spread(1, 1)
+    spread(1)
     wait(res, ar_sem)
 
     @pl.loop(0, COUNT + 3)
@@ -247,7 +278,7 @@
         @pl.when(step < COUNT)
         def _():
             i = step
-            wait(fetched.at[i], gr_sem.at[i])
+            fetched_here(i)
             shared = fetched[i]
             density = jnp.concatenate([shared * res[0], shared * res[1]], axis=1)
             lines = apply_right(density, fwd_z[...])
@@ -267,11 +298,14 @@
 
             c_recv[i, rows(place, block)] = c_send[i, rows(mine, block)]
 
+            @pl.when(step < COUNT - 1)
+            def _():
+                hand_on(step + 1)
+
             @pl.when(step < COUNT - 2)
             def _():
                 select(step + 2)
-                spread(step + 2, 0)
-                spread(step + 2, 1)
+                spread(step + 2)
 
         @pl.when((step >= 1) & (step < COUNT + 1))
         def _():
@@ -399,11 +433,12 @@
     def _(i):
         @pl.when(core == 1 - z % 2)
         def _():
-            wait(fetched.at[i, pl.ds(0, 7 * half)], gs_sem.at[i])
+            wait(fetched.at[i], gs_sem.at[i])
+            wait(fetched.at[i, pl.ds(0, 2 * half)], gs_sem.at[i])
 
         @pl.when(core == z % 2)
         def _():
-            wait(fetched.at[i], gs_sem.at[i])
+            wait(fetched.at[i, pl.ds(0, 5 * half)], gs_sem.at[i])
 
         wait(c_send.at[i, pl.ds(0, block * (GROUP - 1))], cs_sem.at[i])
         wait(d_send.at[i, pl.ds(0, block * (GROUP - 1))], ds_sem.at[i])
@@ -461,7 +496,7 @@
             pltpu.SemaphoreType.DMA((2, 8)),
             sem, sem, sem, sem((2,)), sem((2,)), sem, sem,
         ]
-        + [sems] * 10,
+        + [sems] * 11,
         compiler_params=pltpu.CompilerParams(
             collective_id=0, has_side_effects=True, vmem_limit_bytes=64 * 2**20 - 2**16
         ),

time: 114 us -> 113 us (level)
  no operation moved by 1% of the time
where the time goes in v6:
time: 113 us
  Pallas kernels  112 us (99%)
    pallas_call x1, Pallas kernels, shards(): pl.pallas_call(kernel, out_shape=(jax.ShapeDtypeStruct((2, ROWS, LEN), jn...  110 us

profile of v6, /device:TPU:7, one launch (start us, length us, event | category | flops | bytes accessed | tf_op | source)
XLA Modules:
  0.0 112.8 jit_solution(3354167037927464277)
XLA Ops:
  0.6 110.2 %exchange.1 = (f32[2,512,128]{2,1,0:T(8,128)}, f32[4,4,16,128]{3,2,1,0:T(8,128)}) custom-call(s32[4]{0:T(128)} %owners_in.1, f32[2,512,128]{2,1,0:T(8,128)} %bitcast.3, f32[512,128]{1,0:T(8,128)} %bitcast.4, bf16[768,256]{1,0:T(8,128)(2,1)} %constant.12.clone.fwd_z_in, bf16[256,768]{1,0:T(8,128)(2,1)} %constant.13.clone.fwd_y_in, ...), custom_call_target="tpu_custom_call" | custom-call | tf_op jit(solution)/shard_map/exchange/pallas_call | solution.py:478
  110.9 1.9 %negate.1 = (f32[2,512,128]{2,1,0:T(8,128)}, f32[4,4,16,128]{3,2,1,0:T(8,128)}) custom-call(f32[2,512,128]{2,1,0:T(8,128)} %get-tuple-element.6.exchange, f32[4,4,16,128]{3,2,1,0:T(8,128)} %get-tuple-element.7.projector), custom_call_target="tpu_custom_call" | custom-call | tf_op jit(solution)/shard_map/negate/pallas_call | solution.py:510

commit v7 on v6

--- a/solution.py
+++ b/solution.py
@@ -269,9 +269,9 @@
         load.wait()
 
     hand_on(0)
+    wait(res, ar_sem)
     select(1)
     spread(1)
-    wait(res, ar_sem)
 
     @pl.loop(0, COUNT + 3)
     def _(step):

time: 113 us -> 112 us (level); the launches traced: 113 us -> 110 us
  Pallas kernels: 112 us -> 109 us
    pallas_call x1, Pallas kernels: 110 us -> 107 us  [shards(): pl.pallas_call(kernel, out_shape=(jax.ShapeDtypeStruct((2, ROWS, LEN), jn...]
where the time goes in v7:
time: 112 us; the launch traced here: 110 us
  Pallas kernels  109 us (97%)
    pallas_call x1, Pallas kernels, shards(): pl.pallas_call(kernel, out_shape=(jax.ShapeDtypeStruct((2, ROWS, LEN), jn...  107 us

profile of v7, /device:TPU:7, one launch (start us, length us, event | category | flops | bytes accessed | tf_op | source)
XLA Modules:
  0.0 109.9 jit_solution(15134191389328669081)
XLA Ops:
  0.6 107.4 %exchange.1 = (f32[2,512,128]{2,1,0:T(8,128)}, f32[4,4,16,128]{3,2,1,0:T(8,128)}) custom-call(s32[4]{0:T(128)} %owners_in.1, f32[2,512,128]{2,1,0:T(8,128)} %bitcast.3, f32[512,128]{1,0:T(8,128)} %bitcast.4, bf16[768,256]{1,0:T(8,128)(2,1)} %constant.12.clone.fwd_z_in, bf16[256,768]{1,0:T(8,128)(2,1)} %constant.13.clone.fwd_y_in, ...), custom_call_target="tpu_custom_call" | custom-call | tf_op jit(solution)/shard_map/exchange/pallas_call | solution.py:478
  108.0 1.9 %negate.1 = (f32[2,512,128]{2,1,0:T(8,128)}, f32[4,4,16,128]{3,2,1,0:T(8,128)}) custom-call(f32[2,512,128]{2,1,0:T(8,128)} %get-tuple-element.6.exchange, f32[4,4,16,128]{3,2,1,0:T(8,128)} %get-tuple-element.7.projector), custom_call_target="tpu_custom_call" | custom-call | tf_op jit(solution)/shard_map/negate/pallas_call | solution.py:510

commit v8 on v7

--- a/solution.py
+++ b/solution.py
@@ -471,6 +471,8 @@
     local = pltpu.VMEM((COUNT, ROWS, LEN), jnp.float32)
     pair = pltpu.VMEM((2, ROWS, LEN), jnp.float32)
     single = pltpu.VMEM((ROWS, LEN), jnp.float32)
+    spare = pltpu.VMEM((ROWS + 8, LEN), jnp.float32)
+    wide_spare = pltpu.VMEM((COUNT, GROUP * PLANES * 8 + 8, LEN), jnp.float32)
     tall = pltpu.VMEM((6 * LEN, 2 * LEN), jnp.bfloat16)
     flat = pltpu.VMEM((2 * LEN, 6 * LEN), jnp.bfloat16)
     sem = pltpu.SemaphoreType.DMA
@@ -490,7 +492,7 @@
             pair,
             pltpu.VMEM((2 * BANDS, LEN // 2, LEN), jnp.float32),
             pltpu.VMEM((COUNT, LEN // 2, LEN), jnp.float32),
-            single, local, wide, wide, wide, wide, pair, local,
+            spare, local, wide, wide_spare, wide_spare, wide, pair, local,
             pltpu.VMEM((COUNT, 8, LEN // 2, LEN), jnp.float32),
             pltpu.VMEM((COUNT, LEN // 2, LEN), jnp.float32),
             pltpu.SemaphoreType.DMA((2, 8)),

time: 112 us -> 112 us (level)
  no operation moved by 1% of the time
where the time goes in v8:
time: 112 us; the launch traced here: 110 us
  Pallas kernels  109 us (97%)
    pallas_call x1, Pallas kernels, shards(): pl.pallas_call(kernel, out_shape=(jax.ShapeDtypeStruct((2, ROWS, LEN), jn...  107 us

profile of v8, /device:TPU:7, one launch (start us, length us, event | category | flops | bytes accessed | tf_op | source)
XLA Modules:
  0.0 110.0 jit_solution(17991176635111765342)
XLA Ops:
  0.6 107.4 %exchange.1 = (f32[2,512,128]{2,1,0:T(8,128)}, f32[4,4,16,128]{3,2,1,0:T(8,128)}) custom-call(s32[4]{0:T(128)} %owners_in.1, f32[2,512,128]{2,1,0:T(8,128)} %bitcast.3, f32[512,128]{1,0:T(8,128)} %bitcast.4, bf16[768,256]{1,0:T(8,128)(2,1)} %constant.12.clone.fwd_z_in, bf16[256,768]{1,0:T(8,128)(2,1)} %constant.13.clone.fwd_y_in, ...), custom_call_target="tpu_custom_call" | custom-call | tf_op jit(solution)/shard_map/exchange/pallas_call | solution.py:480
  108.0 1.9 %negate.1 = (f32[2,512,128]{2,1,0:T(8,128)}, f32[4,4,16,128]{3,2,1,0:T(8,128)}) custom-call(f32[2,512,128]{2,1,0:T(8,128)} %get-tuple-element.6.exchange, f32[4,4,16,128]{3,2,1,0:T(8,128)} %get-tuple-element.7.projector), custom_call_target="tpu_custom_call" | custom-call | tf_op jit(solution)/shard_map/negate/pallas_call | solution.py:512

commit v9 on v8

--- a/solution.py
+++ b/solution.py
@@ -117,7 +117,7 @@
              (fwd_x_in, fwd_x), (inv_x_in, inv_x), (inv_y_in, inv_y), (inv_z_in, inv_z)]
         )
     ]
-    for load in loads:
+    for load in loads[:3]:
         load.start()
 
     place = 4 * band + 2 * y_lo + core
@@ -166,6 +166,8 @@
     greet(device((band + 4) % BANDS, y_lo, (band - z + 8) % 8, core))
     for load in loads[:3]:
         load.wait()
+    for load in loads[3:]:
+        load.start()
     total[...] = jnp.zeros_like(total)
     pl.semaphore_wait(barrier, GROUP - 1 + 15 + 1)
 

time: 112 us -> 112 us (level)
  no operation moved by 1% of the time
where the time goes in v9:
time: 112 us; the launch traced here: 110 us
  Pallas kernels  109 us (97%)
    pallas_call x1, Pallas kernels, shards(): pl.pallas_call(kernel, out_shape=(jax.ShapeDtypeStruct((2, ROWS, LEN), jn...  107 us

profile of v9, /device:TPU:7, one launch (start us, length us, event | category | flops | bytes accessed | tf_op | source)
XLA Modules:
  0.0 110.0 jit_solution(695181412531697184)
XLA Ops:
  0.6 107.4 %exchange.1 = (f32[2,512,128]{2,1,0:T(8,128)}, f32[4,4,16,128]{3,2,1,0:T(8,128)}) custom-call(s32[4]{0:T(128)} %owners_in.1, f32[2,512,128]{2,1,0:T(8,128)} %bitcast.3, f32[512,128]{1,0:T(8,128)} %bitcast.4, bf16[768,256]{1,0:T(8,128)(2,1)} %constant.12.clone.fwd_z_in, bf16[256,768]{1,0:T(8,128)(2,1)} %constant.13.clone.fwd_y_in, ...), custom_call_target="tpu_custom_call" | custom-call | tf_op jit(solution)/shard_map/exchange/pallas_call | solution.py:482
  108.0 1.9 %negate.1 = (f32[2,512,128]{2,1,0:T(8,128)}, f32[4,4,16,128]{3,2,1,0:T(8,128)}) custom-call(f32[2,512,128]{2,1,0:T(8,128)} %get-tuple-element.6.exchange, f32[4,4,16,128]{3,2,1,0:T(8,128)} %get-tuple-element.7.projector), custom_call_target="tpu_custom_call" | custom-call | tf_op jit(solution)/shard_map/negate/pallas_call | solution.py:514
